TPU v7x, 512 devices: a whole 4x8x8 slice. The times are simulated.
512 devices in a mesh: blk: 16 (over y, core), grp: 32 (over z, x).
Axes of the slice: x: 4, y: 8, z: 8, core: 2. Of those that a mesh axis runs over, the one named last changes fastest.
Arguments:
- int_table: bfloat16 [16384, 256], P('grp'), may hold values from -0.3984375 to 0.3984375
- dom_rows: int32 [8192, 256], P(('blk', 'grp')), may hold values from 0 to 16383, as said below
- pno_maps: bfloat16 [8192, 256, 128], P(('blk', 'grp')), may hold values from -0.375 to 0.375
- amplitudes: bfloat16 [8192, 128, 128], P(('blk', 'grp')), may hold values from -2.5 to 2.5
- pno_count: int32 [8192], P(('blk', 'grp')), may hold values from 32 to 128
- pno_energy: float32 [8192, 128], P(('blk', 'grp')), may hold values from 0.2 to 3
- occ_sum: float32 [8192], P(('blk', 'grp')), may hold values from -2 to -0.5
- partner_slot: int32 [8192, 6], P(('blk', 'grp')), may hold values from 0 to 47
- margin_index: int32 [8192, 6], P(('blk', 'grp')), may hold values from 0 to 31
- coupling_coef: float32 [8192, 6], P(('blk', 'grp')), may hold values from -0.4 to 0.4
- margin_pool: bfloat16 [1024, 128, 128], P('grp'), may hold values from -0.5 to 0.5
Outputs:
- residual: bfloat16 [8192, 128, 128], P(('blk', 'grp'))
Inputs may be any that keep to these rules, and one draw needn't show every extreme that they name: `dom_rows`: id // 512 is the pair group whose slab holds the row. Among the 4096 entries of one device's pairs no group is named more than 256 times; in every cycle position one group is named exactly 256 times by each device of that position. `partner_slot`: slot w names pair w mod 16 of the slab at cycle position (own position + w // 16 - 1) mod 16 in the same group.
All inputs are finite; a program needn't handle non-finite values.
Results may differ from a plain program's by a relative error of at most 0.0025.
Values may be sent and summed in bfloat16 or wider, within the bound.
No kernel may reach another device: no remote copies, remote signals or barrier semaphores. Data moves between devices by JAX's collectives and lax.ppermute only.
A program may use at most 128 MiB of HBM per device.

v0:
```python
import jax
import jax.numpy as jnp
from jax import lax
from jax.sharding import PartitionSpec as P


def with_halo(cells, sides, width):
    for axis, dim in sides:
        count = lax.axis_size(axis)
        head = lax.slice_in_dim(cells, 0, width, axis=dim)
        tail = lax.slice_in_dim(cells, cells.shape[dim] - width, cells.shape[dim], axis=dim)
        cells = jnp.concatenate(
            [
                lax.ppermute(tail, axis, [(i, (i + 1) % count) for i in range(count)]),
                cells,
                lax.ppermute(head, axis, [((i + 1) % count, i) for i in range(count)]),
            ],
            axis=dim,
        )
    return cells


def couple(tiles, margins, weights):
    half_done = jnp.einsum(
        "pmab,pmbc->pmac", margins, tiles, preferred_element_type=jnp.float32
    ).astype(jnp.bfloat16)
    products = jnp.einsum("pmac,pmdc->pmad", half_done, margins, preferred_element_type=jnp.float32)
    return jnp.einsum("pm,pmad->pad", weights, products, precision=lax.Precision.HIGHEST)


def per_device(
    int_table,
    dom_rows,
    pno_maps,
    amplitudes,
    pno_count,
    pno_energy,
    occ_sum,
    partner_slot,
    margin_index,
    coupling_coef,
    margin_pool,
):
    pairs_here, domain = dom_rows.shape
    row_count, row_width = int_table.shape
    tile_size = amplitudes.shape[1]
    row_ids = dom_rows.reshape(-1)
    whole_table_rows = lax.all_gather(int_table, "grp", axis=0, tiled=True)
    picked = whole_table_rows[row_ids]
    row_block = picked.reshape(pairs_here, domain, row_width)
    projected = jnp.einsum(
        "pqv,pva->pqa", row_block, pno_maps, preferred_element_type=jnp.float32
    ).astype(jnp.bfloat16)
    exchange_k = jnp.einsum(
        "pqa,pqb->pab", projected, projected, preferred_element_type=jnp.float32
    )
    positions = jnp.arange(tile_size, dtype=jnp.int32)
    pno_valid = (positions[None, :] < pno_count[:, None]).astype(jnp.float32)
    tile_mask = pno_valid[:, :, None] * pno_valid[:, None, :]
    masked_amp = jnp.where(tile_mask > 0.5, amplitudes, jnp.zeros_like(amplitudes))
    window = with_halo(masked_amp, (("blk", 0),), pairs_here)
    coupling = couple(window[partner_slot], margin_pool[margin_index], coupling_coef)
    fock_shift = pno_energy[:, :, None] + pno_energy[:, None, :] - occ_sum[:, None, None]
    summed = (exchange_k + fock_shift * amplitudes.astype(jnp.float32) + coupling) * tile_mask
    return summed.astype(jnp.bfloat16)


def solution(mesh):
    placed = (
        P("grp", None),
        P(("blk", "grp"), None),
        P(("blk", "grp"), None, None),
        P(("blk", "grp"), None, None),
        P(("blk", "grp")),
        P(("blk", "grp"), None),
        P(("blk", "grp")),
        P(("blk", "grp"), None),
        P(("blk", "grp"), None),
        P(("blk", "grp"), None),
        P("grp", None, None),
    )
    return jax.shard_map(
        per_device,
        mesh=mesh,
        in_specs=placed,
        out_specs=P(("blk", "grp"), None, None),
        check_vma=False,
    )
```

profile of v0, /device:TPU:1, one launch (start us, length us, event | category | flops | bytes accessed | tf_op | source)
XLA Modules:
  0.0 149.2 jit_solution(13321681756465248443)
XLA Ops:
  6.5 0.7 all-gather.2.cloned.1.call-update
  7.3 0.7 fusion.11
  8.0 1.4 fusion.10
  9.4 2.7 %collective-permute-start = (bf16[16,128,128]{2,1,0:T(8,128)(2,1)S(1)}, bf16[16,128,128]{2,1,0:T(8,128)(2,1)S(1)}, u32[]{:S(2)}, u32[]{:S(2)}) collective-permute-start(bf16[16,128,128]{2,1,0:T(8,128)(2,1)S(1)} %fusion.10), channel_id=1, source_target_pairs={{0,32},{32,64},{64,96},{96,128},{128,160},{160,192},{192,224},{224... | collective-permute-start | bytes 1572872 | tf_op jit(solution)/shard_map/ppermute | solution.py:14
  12.1 4.2 %collective-permute-start.1 = (bf16[16,128,128]{2,1,0:T(8,128)(2,1)S(1)}, bf16[16,128,128]{2,1,0:T(8,128)(2,1)}, u32[]{:S(2)}, u32[]{:S(2)}) collective-permute-start(bf16[16,128,128]{2,1,0:T(8,128)(2,1)S(1)} %fusion.10), channel_id=1, source_target_pairs={{32,0},{64,32},{96,64},{128,96},{160,128},{192,160},{224,192},{256... | collective-permute-start | bytes 1572872 | tf_op jit(solution)/shard_map/ppermute | solution.py:16
  16.3 0.7 copy.22
  17.0 0.7 compare_select_fusion.1
  17.7 0.7 compare_select_fusion.2
  18.4 0.1 copy.17
  18.5 0.1 reshape.95
  18.6 0.1 copy.16
  18.7 0.1 reshape.87
  18.8 0.8 copy.20
  19.6 2.7 %gather_fusion.1 = bf16[96,128,128]{2,1,0:T(8,128)(2,1)} fusion(bf16[32,128,128]{2,1,0:T(8,128)(2,1)S(1)} %copy-done, s32[1024]{0:T(1024)S(1)} %pad_clamp_fusion.1), kind=kCustom, calls=%fused_computation.1 | custom fusion | bytes 6291840 | tf_op jit(solution)/shard_map/gather | solution.py:62
  22.2 0.0 collective-permute-done
  22.3 0.0 copy-start.1
  22.3 0.8 copy-done.1
  23.1 1.4 pad_maximum_fusion
  24.4 2.7 %gather_fusion.2 = bf16[96,128,128]{2,1,0:T(8,128)(2,1)} fusion(bf16[48,128,128]{2,1,0:T(8,128)(2,1)S(1)} %pad_maximum_fusion, s32[1024]{0:T(1024)S(1)} %pad_clamp_fusion), kind=kCustom, calls=%fused_computation.2 | custom fusion | bytes 6291840 | tf_op jit(solution)/shard_map/gather | solution.py:62
  27.1 9.6 %fusion.2 = f32[16,6,128,128]{3,2,1,0:T(8,128)} fusion(bf16[16,6,128,128]{3,2,1,0:T(8,128)(2,1)} %bitcast.17, bf16[16,6,128,128]{3,2,1,0:T(8,128)(2,1)} %bitcast.18), kind=kOutput, calls=%fused_computation.5 | convolution fusion | flops 806879232 | bytes 12582912 | tf_op jit(solution)/shard_map/pmac,pmdc->pmad/dot_general | solution.py:27
  36.7 14.6 %fusion = f32[16,1,128,128]{3,1,2,0:T(1,128)} fusion(f32[16,6,1,1]{1,2,3,0:T(1,128)S(1)} %copy.20, f32[16,6,128,128]{3,2,1,0:T(8,128)} %fusion.2), kind=kOutput, calls=%fused_computation.3 | convolution fusion | flops 18874368 | bytes 7340416 | tf_op jit(solution)/shard_map/pm,pmad->pad/dot_general | solution.py:28
  51.3 68.9 %all-gather.2.cloned.1.call-done = bf16[16384,256]{1,0:T(8,128)(2,1)} async-done(((bf16[512,256]{1,0:T(8,128)(2,1)}), bf16[16384,256]{1,0:T(8,128)(2,1)}) %all-gather.2.cloned.1.call-update) | async-done | bytes 8388624 | tf_op jit(solution)/shard_map/all_gather | solution.py:48
  120.2 17.4 %gather_fusion = bf16[4096,256]{1,0:T(8,128)(2,1)S(1)} fusion(bf16[16384,256]{1,0:T(8,128)(2,1)} %all-gather.2.cloned.1.call-done, s32[4096]{0:T(1024)S(1)} %broadcast_clamp_fusion), kind=kCustom, calls=%fused_computation | custom fusion | bytes 4210688 | tf_op jit(solution)/shard_map/gather | solution.py:49
  137.7 4.7 %fusion.9 = bf16[16,128,128]{2,1,0:T(8,128)(2,1)} fusion(f32[16,128,128]{2,1,0:T(8,128)} %bitcast.20, bf16[16,256,256]{2,1,0:T(8,128)(2,1)S(1)} %bitcast.19, bf16[16,256,128]{2,1,0:T(8,128)(2,1)} %param.13, bf16[16,128,128]{2,1,0:T(8,128)(2,1)} %param.14, f32[16,128]{1,0:T(8,128)S(1)} %fusion.11, f32[16]{0:T(128)S(1)} %copy-done.3, f32[16,128]{1,0:T(8,128)S(1)} %copy-done.2), kind=kOutput, calls=%fused_computation.15 | convolution fusion | flops 405536768 | bytes 5259328 | tf_op jit(solution)/shard_map/pqa,pqb->pab/dot_general | solution.py:54
  (12 shorter events, 0.0 us)
Async XLA Ops:
  6.5 13.0 %copy-start = (bf16[32,128,128]{2,1,0:T(8,128)(2,1)S(1)}, bf16[32,128,128]{2,1,0:T(8,128)(2,1)}, u32[]{:S(2)}) copy-start(bf16[32,128,128]{2,1,0:T(8,128)(2,1)} %param.21) | copy-start | bytes 3145732
  6.5 113.7 %all-gather.2.cloned.1.call-start = ((), (), s32[]{:S(2)}) async-start(), calls=%async_computation | async-start | bytes 8650752 | tf_op jit(solution)/shard_map/all_gather | solution.py:48
  9.4 12.9 %collective-permute-start = (bf16[16,128,128]{2,1,0:T(8,128)(2,1)S(1)}, bf16[16,128,128]{2,1,0:T(8,128)(2,1)S(1)}, u32[]{:S(2)}, u32[]{:S(2)}) collective-permute-start(bf16[16,128,128]{2,1,0:T(8,128)(2,1)S(1)} %fusion.10), channel_id=1, source_target_pairs={{0,32},{32,64},{64,96},{96,128},{128,160},{160,192},{192,224},{224... | collective-permute-start | bytes 1572872 | tf_op jit(solution)/shard_map/ppermute | solution.py:14
  12.1 11.0 %collective-permute-start.1 = (bf16[16,128,128]{2,1,0:T(8,128)(2,1)S(1)}, bf16[16,128,128]{2,1,0:T(8,128)(2,1)}, u32[]{:S(2)}, u32[]{:S(2)}) collective-permute-start(bf16[16,128,128]{2,1,0:T(8,128)(2,1)S(1)} %fusion.10), channel_id=1, source_target_pairs={{32,0},{64,32},{96,64},{128,96},{160,128},{192,160},{224,192},{256... | collective-permute-start | bytes 1572872 | tf_op jit(solution)/shard_map/ppermute | solution.py:16
  22.3 0.8 copy-start.1
  51.3 86.4 %copy-start.2 = (f32[16,128]{1,0:T(8,128)S(1)}, f32[16,128]{1,0:T(8,128)}, u32[]{:S(2)}) copy-start(f32[16,128]{1,0:T(8,128)} %param.16) | copy-start | bytes 24580
  51.3 86.4 %copy-start.3 = (f32[16]{0:T(128)S(1)}, f32[16]{0:T(128)}, u32[]{:S(2)}) copy-start(f32[16]{0:T(128)} %param.17) | copy-start | bytes 196
Sparse Core Ops, SparseCore 0:
  10.5 109.6 all-gather.1
where the time goes:
time: 150 us; the launch traced here: 149 us
  waiting for transfers between devices  69.7 us (46%)
  matrix products  28.9 us (19%)
  local copies, waits for them, and re-layouts  25.4 us (17%)
  between operations  13.5 us (9%)
  starting transfers between devices  6.92 us (5%)
  other arithmetic  4.89 us (3%)
    all_gather x1, waiting for transfers between devices, per_device(): whole_table_rows = lax.all_gather(int_table, 'grp', axis=0, tiled=True)  68.9 us
    gather x1, local copies, waits for them, and re-layouts, per_device(): picked = whole_table_rows[row_ids]  17.4 us
    dot_general x1, matrix products, couple(): jnp.einsum('pm,pmad->pad', weights, products, precision=lax.Precision.HIG...  14.6 us
    dot_general x1, matrix products, couple(): jnp.einsum('pmac,pmdc->pmad', half_done, margins, preferred_element_type=...  9.59 us
    dot_general x1, matrix products, per_device(): jnp.einsum('pqa,pqb->pab', projected, projected, preferred_element_type=j...  4.69 us
    ppermute x1, starting transfers between devices, with_halo(): lax.ppermute(head, axis, [((i + 1) % count, i) for i in range(count)])  4.22 us
  transfers between devices with their start and end apart: 3, of which 1 were waited for; matrix products, arithmetic and copies ran while one was open for 24% of the time, Pallas kernels for 0%

commit v1 on v0

v1 whole, which is shorter than its diff:
```python
import functools

import jax
import jax.numpy as jnp
from jax import lax
from jax.experimental import pallas as pl
from jax.experimental.pallas import tpu as pltpu
from jax.sharding import PartitionSpec as P

NY, NZ, NX = 8, 8, 4
AXES = ("blk", "grp")
SMEM = pl.BlockSpec(memory_space=pltpu.SMEM)
VMEM = pl.BlockSpec(memory_space=pltpu.VMEM)
ANY = pl.BlockSpec(memory_space=pl.ANY)

FETCH = ((4, 2, -2, 0), (3, -3, 1, -1))


def device(y, q, z, x):
    return ((y % NY) * 2 + q) * NZ * NX + (z % NZ) * NX + x % NX


def moves(source):
    places = [(y, q, z, x) for y in range(NY) for q in range(2) for z in range(NZ) for x in range(NX)]
    return [(device(*source(*p)), device(*p)) for p in places]


def fetch_from(step):
    def source(y, q, z, x):
        row = (z + FETCH[q][step]) % NZ
        return y, q, row, x + y + 2 * z - 2 * row + row // 2

    return moves(source)


FETCHES = [fetch_from(step) for step in range(4)]
FROM_NEXT = moves(lambda y, q, z, x: (y, q, z, x + 1) if q == 0 else (y + 1, q, z, x))
FROM_PREVIOUS = moves(lambda y, q, z, x: (y, q, z, x - 1) if q == 0 else (y - 1, q, z, x))
FROM_SIDES = moves(lambda y, q, z, x: (y, q, z + 1, x) if q == 0 else (y, q, z - 1, x))
SWAP = moves(lambda y, q, z, x: (y, 1 - q, z, x))
OUTSIDE = moves(lambda y, q, z, x: (y - 1, 1, z, x) if q == 0 else (y + 1, 0, z, x))


def send(array, pattern):
    return lax.ppermute(array, AXES, pattern)


def spread(own):
    held = [own] + [send(own, pattern) for pattern in (FROM_NEXT, FROM_PREVIOUS, FROM_SIDES)]
    return held + [send(part, SWAP) for part in held]


def places_of(row_ids, shard_rows, y, q, z, x):
    group = row_ids // shard_rows
    row, column = group // NX, group % NX
    step = (column + 2 * row - row // 2 - (x + y + 2 * z)) & 3
    sideways = step == 2
    core = (row - z - sideways.astype(jnp.int32)) & 1
    holder = jnp.where(sideways, jnp.where(core == 0, z + 1, z - 1), z)
    away = (row - holder) & 7
    even = jnp.where(away == 4, 0, jnp.where(away == 2, 1, jnp.where(away == 6, 2, 3)))
    odd = jnp.where(away == 3, 0, jnp.where(away == 5, 1, jnp.where(away == 1, 2, 3)))
    spot = jnp.where(core == 0, even, odd)
    array = jnp.where(step == 0, 0, jnp.where(step == 1, 1, jnp.where(step == 3, 2, 3)))
    return (((core ^ q) * 4 + array) * 4 + spot) * shard_rows + row_ids % shard_rows


def exchange_kernel(pieces, place_ref, count_ref, maps_ref, rest_ref, *refs):
    piece_refs = refs[:pieces]
    out_ref, table_ref, picked, sems = refs[pieces:]
    depth = piece_refs[0].shape[0]
    copies = [
        pltpu.make_async_copy(piece, table_ref.at[pl.ds(i * depth, depth)], sems.at[i])
        for i, piece in enumerate(piece_refs)
    ]
    for copy in copies:
        copy.start()
    for copy in copies:
        copy.wait()
    pairs, _, tile = maps_ref.shape
    domain = place_ref.shape[0] // pairs
    unroll = 32

    @pl.loop(0, pairs * domain // unroll)
    def _(block):
        first = pl.multiple_of(block * 2 * unroll, 2 * unroll)
        for i in range(unroll):
            row = table_ref[place_ref[block * unroll + i]]
            picked[pl.ds(first + 2 * i, 2), :] = row.astype(jnp.float32)

    rows_at = lax.broadcasted_iota(jnp.int32, (tile, tile), 0)
    columns_at = lax.broadcasted_iota(jnp.int32, (tile, tile), 1)
    together = 4

    @pl.loop(0, pairs // together)
    def _(block):
        projected = []
        for i in range(together):
            pair = block * together + i
            first = pl.multiple_of(pair * 2 * domain, 2 * domain)
            low = picked[pl.ds(first, domain, stride=2), :].astype(jnp.bfloat16)
            high = picked[pl.ds(first + 1, domain, stride=2), :].astype(jnp.bfloat16)
            rows = jnp.concatenate([low, high], axis=1)
            projected.append(
                jnp.dot(rows, maps_ref[pair], preferred_element_type=jnp.float32).astype(jnp.bfloat16)
            )
        for i in range(together):
            pair = block * together + i
            gram = lax.dot_general(
                projected[i], projected[i], (((0,), (0,)), ((), ())), preferred_element_type=jnp.float32
            )
            count = count_ref[pair]
            valid = jnp.logical_and(rows_at < count, columns_at < count)
            out_ref[pair] = jnp.where(valid, gram + rest_ref[pair], 0.0).astype(jnp.bfloat16)


def exchange(place, counts, maps, rest, pieces):
    pairs, width, tile = maps.shape
    table_rows = sum(piece.shape[0] for piece in pieces)
    return pl.pallas_call(
        functools.partial(exchange_kernel, len(pieces)),
        out_shape=jax.ShapeDtypeStruct((pairs, tile, tile), jnp.bfloat16),
        in_specs=[SMEM, SMEM, VMEM, VMEM] + [ANY] * len(pieces),
        out_specs=VMEM,
        scratch_shapes=[
            pltpu.VMEM((table_rows, 2, width // 2), jnp.bfloat16),
            pltpu.VMEM((place.shape[0] * 2, width // 2), jnp.float32),
            pltpu.SemaphoreType.DMA((len(pieces),)),
        ],
        compiler_params=pltpu.CompilerParams(vmem_limit_bytes=32 * 2**20),
        cost_estimate=pl.CostEstimate(flops=10**9, bytes_accessed=30 * 2**20, transcendentals=0),
    )(place, counts, maps, rest, *pieces)


def couple_kernel(
    slot_ref, margin_ref, coef_ref, occ_ref, energy_ref, outside_ref, own_ref, partner_ref, pool_ref, out_ref, window, sems
):
    pairs, parts = slot_ref.shape
    tile = own_ref.shape[1]
    copies = [
        pltpu.make_async_copy(tiles, window.at[pl.ds(i * pairs, pairs)], sems.at[i])
        for i, tiles in enumerate((outside_ref, own_ref, partner_ref))
    ]
    for copy in copies:
        copy.start()
    for copy in copies:
        copy.wait()
    together = 2

    @pl.loop(0, pairs // together)
    def _(block):
        halves = []
        for i in range(together):
            pair = block * together + i
            for m in range(parts):
                margin = pool_ref[margin_ref[pair, m]]
                half = jnp.dot(margin, window[slot_ref[pair, m]], preferred_element_type=jnp.float32)
                halves.append((half.astype(jnp.bfloat16), margin))
        for i in range(together):
            pair = block * together + i
            energy = jnp.broadcast_to(energy_ref[pl.ds(pair, 1), :], (tile, tile))
            shift = energy + jnp.swapaxes(energy, 0, 1) - occ_ref[pair]
            total = shift * window[pairs + pair].astype(jnp.float32)
            for m in range(parts):
                half, margin = halves[i * parts + m]
                product = lax.dot_general(
                    half, margin, (((1,), (1,)), ((), ())), preferred_element_type=jnp.float32
                )
                total += coef_ref[pair, m] * product
            out_ref[pair] = total


def couple(slot, margin, coef, occ, energy, outside, own, partner, pool):
    pairs, tile, _ = own.shape
    return pl.pallas_call(
        couple_kernel,
        out_shape=jax.ShapeDtypeStruct((pairs, tile, tile), jnp.float32),
        in_specs=[SMEM] * 4 + [VMEM] + [ANY] * 3 + [VMEM],
        out_specs=VMEM,
        scratch_shapes=[
            pltpu.VMEM((3 * pairs, tile, tile), jnp.bfloat16),
            pltpu.SemaphoreType.DMA((3,)),
        ],
        compiler_params=pltpu.CompilerParams(vmem_limit_bytes=16 * 2**20),
        cost_estimate=pl.CostEstimate(flops=10**9, bytes_accessed=20 * 2**20, transcendentals=0),
    )(slot, margin, coef, occ, energy, outside, own, partner, pool)


def per_device(
    int_table,
    dom_rows,
    pno_maps,
    amplitudes,
    pno_count,
    pno_energy,
    occ_sum,
    partner_slot,
    margin_index,
    coupling_coef,
    margin_pool,
):
    shard_rows, width = int_table.shape
    pairs, tile, _ = amplitudes.shape
    blk, grp = lax.axis_index("blk"), lax.axis_index("grp")
    y, q, z, x = blk // 2, blk % 2, grp // NX, grp % NX

    shard = int_table.reshape(shard_rows, 2, width // 2)
    valid = jnp.arange(tile, dtype=jnp.int32)[None, :] < pno_count[:, None]
    mask = jnp.logical_and(valid[:, :, None], valid[:, None, :])
    masked = jnp.where(mask, amplitudes, jnp.zeros_like(amplitudes))

    fetched = [send(shard, pattern) for pattern in FETCHES[:2]]
    shard, masked = lax.optimization_barrier((shard, masked))
    outside = send(masked, OUTSIDE)
    fetched += [send(shard, pattern) for pattern in FETCHES[2:]]
    partner = send(masked, SWAP)
    part = partner_slot // pairs
    slot = jnp.where(q == 0, part, 2 - part) * pairs + partner_slot % pairs
    rest = couple(
        slot, margin_index, coupling_coef, occ_sum, pno_energy, outside, masked, partner, margin_pool
    )
    place = places_of(dom_rows, shard_rows, y, q, z, x).reshape(-1)
    fetched, rest, place = lax.optimization_barrier((fetched, rest, place))
    return exchange(place, pno_count, pno_maps, rest, spread(jnp.concatenate(fetched, axis=0)))


def solution(mesh):
    pairs = P(AXES)
    return jax.shard_map(
        per_device,
        mesh=mesh,
        in_specs=(P("grp"),) + (pairs,) * 9 + (P("grp"),),
        out_specs=pairs,
        check_vma=False,
    )
```

time: 150 us -> 89.5 us (0.60)
  waiting for transfers between devices: 69.7 us -> 11 us
  starting transfers between devices: 6.92 us -> 57.8 us
  matrix products: 28.9 us -> 0 us
  local copies, waits for them, and re-layouts: 25.4 us -> 4.99 us
  Pallas kernels: 0 us -> 13.5 us
  between operations: 13.5 us -> 0.32 us
  other arithmetic: 4.89 us -> 1.28 us
    all_gather x1 -> x0, waiting for transfers between devices: 68.9 us -> none  [per_device(): whole_table_rows = lax.all_gather(int_table, 'grp', axis=0, tiled=True)]
    ppermute x2 -> x13, starting transfers between devices: 6.92 us -> 57.8 us  [send(): return lax.ppermute(array, AXES, pattern)]
    dot_general x3 -> x0, matrix products: 28.9 us -> none  [the longest x1 14.6 us: couple(): jnp.einsum('pm,pmad->pad', weights, products, precision=lax.Precision.HIG...]
    gather x3 -> x0, local copies, waits for them, and re-layouts: 22.8 us -> none  [the longest x1 17.4 us: per_device(): picked = whole_table_rows[row_ids]]
    pallas_call x0 -> x2, Pallas kernels: none -> 13.5 us  [the longest x1 8.21 us: exchange(): pl.pallas_call(functools.partial(exchange_kernel, len(pieces)), out_shape...]
    ppermute x2 -> x13, waiting for transfers between devices: 0.01 us -> 11 us  [send(): return lax.ppermute(array, AXES, pattern)]
    select_n x4 -> x1, other arithmetic: 2.78 us -> 0.34 us  [per_device(): masked = jnp.where(mask, amplitudes, jnp.zeros_like(amplitudes))]
    unnamed x10 -> x27, local copies, waits for them, and re-layouts: 2.3 us -> 3.76 us
  transfers between devices with their start and end apart: 3 -> 13, of which waited for: 1 -> 5; matrix products, arithmetic and copies ran while one was open for 24% -> 0% of each run, Pallas kernels for 0% -> 6%
where the time goes in v1:
time: 89.5 us; the launch traced here: 88.9 us
  starting transfers between devices  57.8 us (65%)
  Pallas kernels  13.5 us (15%)
  waiting for transfers between devices  11 us (12%)
  local copies, waits for them, and re-layouts  4.99 us (6%)
  other arithmetic  1.28 us (1%)
    ppermute x13, starting transfers between devices, send(): return lax.ppermute(array, AXES, pattern)  57.8 us
    ppermute x13, waiting for transfers between devices, send(): return lax.ppermute(array, AXES, pattern)  11 us
    pallas_call x1, Pallas kernels, exchange(): pl.pallas_call(functools.partial(exchange_kernel, len(pieces)), out_shape...  8.21 us
    pallas_call x1, Pallas kernels, couple(): pl.pallas_call(couple_kernel, out_shape=jax.ShapeDtypeStruct((pairs, tile...  5.33 us
    unnamed x27, local copies, waits for them, and re-layouts  3.76 us
  transfers between devices with their start and end apart: 13, of which 5 were waited for; matrix products, arithmetic and copies ran while one was open for 0% of the time, Pallas kernels for 6%

profile of v1, /device:TPU:1, one launch (start us, length us, event | category | flops | bytes accessed | tf_op | source)
XLA Modules:
  0.0 88.9 jit_solution(16559648904196080365)
XLA Ops:
  0.0 0.8 iota_compare_fusion
  0.9 1.0 %reshape.42 = bf16[512,2,128]{2,1,0:T(2,128)(2,1)S(1)} reshape(bf16[512,256]{1,0:T(8,128)(2,1)} %param.11) | data formatting | bytes 524288 | tf_op jit(solution)/shard_map/reshape | solution.py:207
  2.2 8.8 %collective-permute-start.5 = (bf16[16,128,128]{2,1,0:T(8,128)(2,1)S(1)}, bf16[16,128,128]{2,1,0:T(8,128)(2,1)S(1)}, u32[]{:S(2)}, u32[]{:S(2)}) collective-permute-start(bf16[16,128,128]{2,1,0:T(8,128)(2,1)S(1)} %and_select_fusion.own_ref), channel_id=1, source_target_pairs={{32,0},{33,1},{34,2},{35,3},{36,4},{37,5},{38,6},{39,7},{40,8},{41... | collective-permute-start | bytes 1572872 | tf_op jit(solution)/shard_map/ppermute | solution.py:45
  11.0 1.9 %collective-permute-start.4 = (bf16[16,128,128]{2,1,0:T(8,128)(2,1)S(1)}, bf16[16,128,128]{2,1,0:T(8,128)(2,1)S(1)}, u32[]{:S(2)}, u32[]{:S(2)}) collective-permute-start(bf16[16,128,128]{2,1,0:T(8,128)(2,1)S(1)} %and_select_fusion.own_ref), channel_id=1, source_target_pairs={{480,0},{481,1},{482,2},{483,3},{484,4},{485,5},{486,6},{487,7},{4... | collective-permute-start | bytes 1572872 | tf_op jit(solution)/shard_map/ppermute | solution.py:45
  12.9 5.9 %collective-permute-start.1 = (bf16[512,2,128]{2,1,0:T(2,128)(2,1)S(1)}, bf16[512,2,128]{2,1,0:T(2,128)(2,1)S(1)}, u32[]{:S(2)}, u32[]{:S(2)}) collective-permute-start(bf16[512,2,128]{2,1,0:T(2,128)(2,1)S(1)} %reshape.42), channel_id=1, source_target_pairs={{9,0},{10,1},{11,2},{8,3},{13,4},{14,5},{15,6},{12,7},{18,8},{19,9... | collective-permute-start | bytes 786440 | tf_op jit(solution)/shard_map/ppermute | solution.py:45
  18.8 5.0 %collective-permute-start = (bf16[512,2,128]{2,1,0:T(2,128)(2,1)S(1)}, bf16[512,2,128]{2,1,0:T(2,128)(2,1)}, u32[]{:S(2)}, u32[]{:S(2)}) collective-permute-start(bf16[512,2,128]{2,1,0:T(2,128)(2,1)S(1)} %reshape.42), channel_id=1, source_target_pairs={{18,0},{19,1},{16,2},{17,3},{22,4},{23,5},{20,6},{21,7},{27,8},{24... | collective-permute-start | bytes 786440 | tf_op jit(solution)/shard_map/ppermute | solution.py:45
  23.8 3.0 %collective-permute-start.3 = (bf16[512,2,128]{2,1,0:T(2,128)(2,1)S(1)}, bf16[512,2,128]{2,1,0:T(2,128)(2,1)S(1)}, u32[]{:S(2)}, u32[]{:S(2)}) collective-permute-start(bf16[512,2,128]{2,1,0:T(2,128)(2,1)S(1)} %reshape.42), channel_id=1, source_target_pairs={{0,0},{1,1},{2,2},{3,3},{4,4},{5,5},{6,6},{7,7},{9,8},{10,9},{11,1... | collective-permute-start | bytes 786440 | tf_op jit(solution)/shard_map/ppermute | solution.py:45
  26.9 0.7 copy-done.7
  27.7 0.6 copy-done.8
  29.1 5.0 %collective-permute-start.2 = (bf16[512,2,128]{2,1,0:T(2,128)(2,1)S(1)}, bf16[512,2,128]{2,1,0:T(2,128)(2,1)S(1)}, u32[]{:S(2)}, u32[]{:S(2)}) collective-permute-start(bf16[512,2,128]{2,1,0:T(2,128)(2,1)S(1)} %reshape.42), channel_id=1, source_target_pairs={{27,0},{24,1},{25,2},{26,3},{31,4},{28,5},{29,6},{30,7},{0,8},{1,9... | collective-permute-start | bytes 786440 | tf_op jit(solution)/shard_map/ppermute | solution.py:45
  34.2 5.3 %shard_map.109.rest_ref = f32[16,128,128]{2,1,0:T(8,128)S(1)} custom-call(s32[16,6]{1,0:T(8,128)S(1)} %fusion.12.slot_ref, s32[16,6]{1,0:T(8,128)S(1)} %copy.16.margin_ref, f32[16,6]{1,0:T(8,128)S(1)} %copy.17.coef_ref, f32[16]{0:T(128)S(1)} %copy-done.4, f32[16,128]{1,0:T(8,128)S(1)} %copy-done.2, ...), custom_call_target="tpu_custom_call" | custom-call | flops 1000000000 | bytes 20971520 | tf_op jit(solution)/shard_map/pallas_call | solution.py:175
  39.5 2.4 %collective-permute-done = bf16[512,2,128]{2,1,0:T(2,128)(2,1)} collective-permute-done((bf16[512,2,128]{2,1,0:T(2,128)(2,1)S(1)}, bf16[512,2,128]{2,1,0:T(2,128)(2,1)}, u32[]{:S(2)}, u32[]{:S(2)}) %collective-permute-start) | collective-permute-done | bytes 262176 | tf_op jit(solution)/shard_map/ppermute | solution.py:45
  41.9 3.9 %collective-permute-done.2 = bf16[512,2,128]{2,1,0:T(2,128)(2,1)S(1)} collective-permute-done((bf16[512,2,128]{2,1,0:T(2,128)(2,1)S(1)}, bf16[512,2,128]{2,1,0:T(2,128)(2,1)S(1)}, u32[]{:S(2)}, u32[]{:S(2)}) %collective-permute-start.2) | collective-permute-done | bytes 262176 | tf_op jit(solution)/shard_map/ppermute | solution.py:45
  45.8 1.2 %constant_dynamic-update-slice_fusion.3 = bf16[2048,2,128]{2,1,0:T(2,128)(2,1)S(1)} fusion(bf16[512,2,128]{2,1,0:T(2,128)(2,1)} %collective-permute-done), kind=kLoop, calls=%fused_computation.40 | loop fusion | bytes 524288
  47.7 1.9 %collective-permute-start.8 = (bf16[2048,2,128]{2,1,0:T(2,128)(2,1)S(1)}, bf16[2048,2,128]{2,1,0:T(2,128)(2,1)S(1)}, u32[]{:S(2)}, u32[]{:S(2)}) collective-permute-start(bf16[2048,2,128]{2,1,0:T(2,128)(2,1)S(1)} %constant_dynamic-update-slice_fusion.refs_0_), channel_id=1, source_target_pairs={{4,0},{5,1},{6,2},{7,3},{8,4},{9,5},{10,6},{11,7},{12,8},{13,9},{1... | collective-permute-start | bytes 3145736 | tf_op jit(solution)/shard_map/ppermute | solution.py:45
  49.6 2.8 %collective-permute-start.7 = (bf16[2048,2,128]{2,1,0:T(2,128)(2,1)S(1)}, bf16[2048,2,128]{2,1,0:T(2,128)(2,1)S(1)}, u32[]{:S(2)}, u32[]{:S(2)}) collective-permute-start(bf16[2048,2,128]{2,1,0:T(2,128)(2,1)S(1)} %constant_dynamic-update-slice_fusion.refs_0_), channel_id=1, source_target_pairs={{3,0},{0,1},{1,2},{2,3},{7,4},{4,5},{5,6},{6,7},{11,8},{8,9},{9,10... | collective-permute-start | bytes 3145736 | tf_op jit(solution)/shard_map/ppermute | solution.py:45
  52.4 3.7 %collective-permute-start.6 = (bf16[2048,2,128]{2,1,0:T(2,128)(2,1)S(1)}, bf16[2048,2,128]{2,1,0:T(2,128)(2,1)S(1)}, u32[]{:S(2)}, u32[]{:S(2)}) collective-permute-start(bf16[2048,2,128]{2,1,0:T(2,128)(2,1)S(1)} %constant_dynamic-update-slice_fusion.refs_0_), channel_id=1, source_target_pairs={{1,0},{2,1},{3,2},{0,3},{5,4},{6,5},{7,6},{4,7},{9,8},{10,9},{11,1... | collective-permute-start | bytes 3145736 | tf_op jit(solution)/shard_map/ppermute | solution.py:45
  56.1 9.1 %collective-permute-start.9 = (bf16[2048,2,128]{2,1,0:T(2,128)(2,1)S(1)}, bf16[2048,2,128]{2,1,0:T(2,128)(2,1)S(1)}, u32[]{:S(2)}, u32[]{:S(2)}) collective-permute-start(bf16[2048,2,128]{2,1,0:T(2,128)(2,1)S(1)} %constant_dynamic-update-slice_fusion.refs_0_), channel_id=1, source_target_pairs={{32,0},{33,1},{34,2},{35,3},{36,4},{37,5},{38,6},{39,7},{40,8},{41... | collective-permute-start | bytes 3145736 | tf_op jit(solution)/shard_map/ppermute | solution.py:45
  65.3 2.0 %collective-permute-done.8.refs_3_ = bf16[2048,2,128]{2,1,0:T(2,128)(2,1)S(1)} collective-permute-done((bf16[2048,2,128]{2,1,0:T(2,128)(2,1)S(1)}, bf16[2048,2,128]{2,1,0:T(2,128)(2,1)S(1)}, u32[]{:S(2)}, u32[]{:S(2)}) %collective-permute-start.8) | collective-permute-done | bytes 1048608 | tf_op jit(solution)/shard_map/ppermute | solution.py:45
  67.3 3.2 %collective-permute-start.12 = (bf16[2048,2,128]{2,1,0:T(2,128)(2,1)S(1)}, bf16[2048,2,128]{2,1,0:T(2,128)(2,1)S(1)}, u32[]{:S(2)}, u32[]{:S(2)}) collective-permute-start(bf16[2048,2,128]{2,1,0:T(2,128)(2,1)S(1)} %collective-permute-done.8.refs_3_), channel_id=1, source_target_pairs={{32,0},{33,1},{34,2},{35,3},{36,4},{37,5},{38,6},{39,7},{40,8},{41... | collective-permute-start | bytes 3145736 | tf_op jit(solution)/shard_map/ppermute | solution.py:45
  70.5 5.6 %collective-permute-start.11 = (bf16[2048,2,128]{2,1,0:T(2,128)(2,1)S(1)}, bf16[2048,2,128]{2,1,0:T(2,128)(2,1)S(1)}, u32[]{:S(2)}, u32[]{:S(2)}) collective-permute-start(bf16[2048,2,128]{2,1,0:T(2,128)(2,1)S(1)} %collective-permute-done.7.refs_2_), channel_id=1, source_target_pairs={{32,0},{33,1},{34,2},{35,3},{36,4},{37,5},{38,6},{39,7},{40,8},{41... | collective-permute-start | bytes 3145736 | tf_op jit(solution)/shard_map/ppermute | solution.py:45
  76.1 1.9 %collective-permute-start.10 = (bf16[2048,2,128]{2,1,0:T(2,128)(2,1)S(1)}, bf16[2048,2,128]{2,1,0:T(2,128)(2,1)S(1)}, u32[]{:S(2)}, u32[]{:S(2)}) collective-permute-start(bf16[2048,2,128]{2,1,0:T(2,128)(2,1)S(1)} %collective-permute-done.6.refs_1_), channel_id=1, source_target_pairs={{32,0},{33,1},{34,2},{35,3},{36,4},{37,5},{38,6},{39,7},{40,8},{41... | collective-permute-start | bytes 3145736 | tf_op jit(solution)/shard_map/ppermute | solution.py:45
  78.4 2.3 %collective-permute-done.10.refs_5_ = bf16[2048,2,128]{2,1,0:T(2,128)(2,1)S(1)} collective-permute-done((bf16[2048,2,128]{2,1,0:T(2,128)(2,1)S(1)}, bf16[2048,2,128]{2,1,0:T(2,128)(2,1)S(1)}, u32[]{:S(2)}, u32[]{:S(2)}) %collective-permute-start.10) | collective-permute-done | bytes 1048608 | tf_op jit(solution)/shard_map/ppermute | solution.py:45
  80.7 8.2 %shard_map.110 = bf16[16,128,128]{2,1,0:T(8,128)(2,1)} custom-call(s32[4096]{0:T(1024)S(1)} %bitcast.3, s32[16]{0:T(128)S(1)} %copy-done.3, bf16[16,256,128]{2,1,0:T(8,128)(2,1)S(1)} %copy-done.1, f32[16,128,128]{2,1,0:T(8,128)S(1)} %shard_map.109.rest_ref, bf16[2048,2,128]{2,1,0:T(2,128)(2,1)S(1)} %constant_dynamic-update-slice_fusion.refs_0_, ...), custom_call_target="tpu_custom_call" | custom-call | flops 1000000000 | bytes 31457280 | tf_op jit(solution)/shard_map/pallas_call | solution.py:120
  (37 shorter events, 2.3 us)
Async XLA Ops:
  0.0 1.9 %copy-start.5 = (bf16[16,128,128]{2,1,0:T(8,128)(2,1)S(1)}, bf16[16,128,128]{2,1,0:T(8,128)(2,1)}, u32[]{:S(2)}) copy-start(bf16[16,128,128]{2,1,0:T(8,128)(2,1)} %param.14) | copy-start | bytes 1572868
  0.0 34.1 %copy-start = (bf16[32,128,128]{2,1,0:T(8,128)(2,1)S(1)}, bf16[32,128,128]{2,1,0:T(8,128)(2,1)}, u32[]{:S(2)}) copy-start(bf16[32,128,128]{2,1,0:T(8,128)(2,1)} %pool_ref.1) | copy-start | bytes 3145732
  2.2 26.9 %collective-permute-start.5 = (bf16[16,128,128]{2,1,0:T(8,128)(2,1)S(1)}, bf16[16,128,128]{2,1,0:T(8,128)(2,1)S(1)}, u32[]{:S(2)}, u32[]{:S(2)}) collective-permute-start(bf16[16,128,128]{2,1,0:T(8,128)(2,1)S(1)} %and_select_fusion.own_ref), channel_id=1, source_target_pairs={{32,0},{33,1},{34,2},{35,3},{36,4},{37,5},{38,6},{39,7},{40,8},{41... | collective-permute-start | bytes 1572872 | tf_op jit(solution)/shard_map/ppermute | solution.py:45
  11.0 23.1 %collective-permute-start.4 = (bf16[16,128,128]{2,1,0:T(8,128)(2,1)S(1)}, bf16[16,128,128]{2,1,0:T(8,128)(2,1)S(1)}, u32[]{:S(2)}, u32[]{:S(2)}) collective-permute-start(bf16[16,128,128]{2,1,0:T(8,128)(2,1)S(1)} %and_select_fusion.own_ref), channel_id=1, source_target_pairs={{480,0},{481,1},{482,2},{483,3},{484,4},{485,5},{486,6},{487,7},{4... | collective-permute-start | bytes 1572872 | tf_op jit(solution)/shard_map/ppermute | solution.py:45
  12.9 26.6 %collective-permute-start.1 = (bf16[512,2,128]{2,1,0:T(2,128)(2,1)S(1)}, bf16[512,2,128]{2,1,0:T(2,128)(2,1)S(1)}, u32[]{:S(2)}, u32[]{:S(2)}) collective-permute-start(bf16[512,2,128]{2,1,0:T(2,128)(2,1)S(1)} %reshape.42), channel_id=1, source_target_pairs={{9,0},{10,1},{11,2},{8,3},{13,4},{14,5},{15,6},{12,7},{18,8},{19,9... | collective-permute-start | bytes 786440 | tf_op jit(solution)/shard_map/ppermute | solution.py:45
  18.8 23.1 %collective-permute-start = (bf16[512,2,128]{2,1,0:T(2,128)(2,1)S(1)}, bf16[512,2,128]{2,1,0:T(2,128)(2,1)}, u32[]{:S(2)}, u32[]{:S(2)}) collective-permute-start(bf16[512,2,128]{2,1,0:T(2,128)(2,1)S(1)} %reshape.42), channel_id=1, source_target_pairs={{18,0},{19,1},{16,2},{17,3},{22,4},{23,5},{20,6},{21,7},{27,8},{24... | collective-permute-start | bytes 786440 | tf_op jit(solution)/shard_map/ppermute | solution.py:45
  23.8 18.1 %collective-permute-start.3 = (bf16[512,2,128]{2,1,0:T(2,128)(2,1)S(1)}, bf16[512,2,128]{2,1,0:T(2,128)(2,1)S(1)}, u32[]{:S(2)}, u32[]{:S(2)}) collective-permute-start(bf16[512,2,128]{2,1,0:T(2,128)(2,1)S(1)} %reshape.42), channel_id=1, source_target_pairs={{0,0},{1,1},{2,2},{3,3},{4,4},{5,5},{6,6},{7,7},{9,8},{10,9},{11,1... | collective-permute-start | bytes 786440 | tf_op jit(solution)/shard_map/ppermute | solution.py:45
  26.9 0.7 copy-start.7
  26.9 1.5 %copy-start.9 = (f32[16,6]{0,1:T(8,128)S(1)}, f32[16,6]{0,1:T(8,128)}, u32[]{:S(2)}) copy-start(f32[16,6]{0,1:T(8,128)} %param.20) | copy-start | bytes 1156
  27.6 0.7 copy-start.8
  28.3 0.7 copy-start.6
  29.1 5.1 %copy-start.2 = (f32[16,128]{1,0:T(8,128)S(1)}, f32[16,128]{1,0:T(8,128)}, u32[]{:S(2)}) copy-start(f32[16,128]{1,0:T(8,128)} %energy_ref.1) | copy-start | bytes 24580
  29.1 5.1 %copy-start.4 = (f32[16]{0:T(128)S(1)}, f32[16]{0:T(128)}, u32[]{:S(2)}) copy-start(f32[16]{0:T(128)} %occ_ref.1) | copy-start | bytes 196
  29.1 16.7 %collective-permute-start.2 = (bf16[512,2,128]{2,1,0:T(2,128)(2,1)S(1)}, bf16[512,2,128]{2,1,0:T(2,128)(2,1)S(1)}, u32[]{:S(2)}, u32[]{:S(2)}) collective-permute-start(bf16[512,2,128]{2,1,0:T(2,128)(2,1)S(1)} %reshape.42), channel_id=1, source_target_pairs={{27,0},{24,1},{25,2},{26,3},{31,4},{28,5},{29,6},{30,7},{0,8},{1,9... | collective-permute-start | bytes 786440 | tf_op jit(solution)/shard_map/ppermute | solution.py:45
  45.8 34.9 %copy-start.1 = (bf16[16,256,128]{2,1,0:T(8,128)(2,1)S(1)}, bf16[16,256,128]{2,1,0:T(8,128)(2,1)}, u32[]{:S(2)}) copy-start(bf16[16,256,128]{2,1,0:T(8,128)(2,1)} %maps_ref.1) | copy-start | bytes 3145732
  47.5 33.2 %copy-start.3 = (s32[16]{0:T(128)S(1)}, s32[16]{0:T(128)}, u32[]{:S(2)}) copy-start(s32[16]{0:T(128)} %count_ref.1) | copy-start | bytes 196
  47.7 19.6 %collective-permute-start.8 = (bf16[2048,2,128]{2,1,0:T(2,128)(2,1)S(1)}, bf16[2048,2,128]{2,1,0:T(2,128)(2,1)S(1)}, u32[]{:S(2)}, u32[]{:S(2)}) collective-permute-start(bf16[2048,2,128]{2,1,0:T(2,128)(2,1)S(1)} %constant_dynamic-update-slice_fusion.refs_0_), channel_id=1, source_target_pairs={{4,0},{5,1},{6,2},{7,3},{8,4},{9,5},{10,6},{11,7},{12,8},{13,9},{1... | collective-permute-start | bytes 3145736 | tf_op jit(solution)/shard_map/ppermute | solution.py:45
  49.6 20.9 %collective-permute-start.7 = (bf16[2048,2,128]{2,1,0:T(2,128)(2,1)S(1)}, bf16[2048,2,128]{2,1,0:T(2,128)(2,1)S(1)}, u32[]{:S(2)}, u32[]{:S(2)}) collective-permute-start(bf16[2048,2,128]{2,1,0:T(2,128)(2,1)S(1)} %constant_dynamic-update-slice_fusion.refs_0_), channel_id=1, source_target_pairs={{3,0},{0,1},{1,2},{2,3},{7,4},{4,5},{5,6},{6,7},{11,8},{8,9},{9,10... | collective-permute-start | bytes 3145736 | tf_op jit(solution)/shard_map/ppermute | solution.py:45
  52.4 23.7 %collective-permute-start.6 = (bf16[2048,2,128]{2,1,0:T(2,128)(2,1)S(1)}, bf16[2048,2,128]{2,1,0:T(2,128)(2,1)S(1)}, u32[]{:S(2)}, u32[]{:S(2)}) collective-permute-start(bf16[2048,2,128]{2,1,0:T(2,128)(2,1)S(1)} %constant_dynamic-update-slice_fusion.refs_0_), channel_id=1, source_target_pairs={{1,0},{2,1},{3,2},{0,3},{5,4},{6,5},{7,6},{4,7},{9,8},{10,9},{11,1... | collective-permute-start | bytes 3145736 | tf_op jit(solution)/shard_map/ppermute | solution.py:45
  56.1 21.9 %collective-permute-start.9 = (bf16[2048,2,128]{2,1,0:T(2,128)(2,1)S(1)}, bf16[2048,2,128]{2,1,0:T(2,128)(2,1)S(1)}, u32[]{:S(2)}, u32[]{:S(2)}) collective-permute-start(bf16[2048,2,128]{2,1,0:T(2,128)(2,1)S(1)} %constant_dynamic-update-slice_fusion.refs_0_), channel_id=1, source_target_pairs={{32,0},{33,1},{34,2},{35,3},{36,4},{37,5},{38,6},{39,7},{40,8},{41... | collective-permute-start | bytes 3145736 | tf_op jit(solution)/shard_map/ppermute | solution.py:45
  67.3 10.7 %collective-permute-start.12 = (bf16[2048,2,128]{2,1,0:T(2,128)(2,1)S(1)}, bf16[2048,2,128]{2,1,0:T(2,128)(2,1)S(1)}, u32[]{:S(2)}, u32[]{:S(2)}) collective-permute-start(bf16[2048,2,128]{2,1,0:T(2,128)(2,1)S(1)} %collective-permute-done.8.refs_3_), channel_id=1, source_target_pairs={{32,0},{33,1},{34,2},{35,3},{36,4},{37,5},{38,6},{39,7},{40,8},{41... | collective-permute-start | bytes 3145736 | tf_op jit(solution)/shard_map/ppermute | solution.py:45
  70.5 7.9 %collective-permute-start.11 = (bf16[2048,2,128]{2,1,0:T(2,128)(2,1)S(1)}, bf16[2048,2,128]{2,1,0:T(2,128)(2,1)S(1)}, u32[]{:S(2)}, u32[]{:S(2)}) collective-permute-start(bf16[2048,2,128]{2,1,0:T(2,128)(2,1)S(1)} %collective-permute-done.7.refs_2_), channel_id=1, source_target_pairs={{32,0},{33,1},{34,2},{35,3},{36,4},{37,5},{38,6},{39,7},{40,8},{41... | collective-permute-start | bytes 3145736 | tf_op jit(solution)/shard_map/ppermute | solution.py:45
  76.1 4.6 %collective-permute-start.10 = (bf16[2048,2,128]{2,1,0:T(2,128)(2,1)S(1)}, bf16[2048,2,128]{2,1,0:T(2,128)(2,1)S(1)}, u32[]{:S(2)}, u32[]{:S(2)}) collective-permute-start(bf16[2048,2,128]{2,1,0:T(2,128)(2,1)S(1)} %collective-permute-done.6.refs_1_), channel_id=1, source_target_pairs={{32,0},{33,1},{34,2},{35,3},{36,4},{37,5},{38,6},{39,7},{40,8},{41... | collective-permute-start | bytes 3145736 | tf_op jit(solution)/shard_map/ppermute | solution.py:45

commit v2 on v1

v2 whole, which is shorter than its diff:
```python
import functools

import jax
import jax.numpy as jnp
from jax import lax
from jax.experimental import pallas as pl
from jax.experimental.pallas import tpu as pltpu
from jax.sharding import PartitionSpec as P

NY, NZ, NX = 8, 8, 4
AXES = ("blk", "grp")
SMEM = pl.BlockSpec(memory_space=pltpu.SMEM)
VMEM = pl.BlockSpec(memory_space=pltpu.VMEM)
ANY = pl.BlockSpec(memory_space=pl.ANY)
HBM = pl.BlockSpec(memory_space=pltpu.HBM)

FETCH = ((0, 2), (1, 3))
TILT = 2


def device(y, q, z, x):
    return ((y % NY) * 2 + q) * NZ * NX + (z % NZ) * NX + x % NX


def moves(source):
    places = [(y, q, z, x) for y in range(NY) for q in range(2) for z in range(NZ) for x in range(NX)]
    return [(device(*source(*p)), device(*p)) for p in places]


def fetch_from(step):
    def source(y, q, z, x):
        colour = (2 * x + y + 3 * z) % 8
        number = (z // 2 + FETCH[q][step]) % 4
        return y, q, 2 * number + colour % 2, colour // 2 + TILT * number

    return moves(source)


FETCHES = [fetch_from(step) for step in range(2)]
FROM_X = moves(lambda y, q, z, x: (y, q, z, x + 1 - 2 * q))
FROM_Y = moves(lambda y, q, z, x: (y + 1 - 2 * q, q, z, x))
FROM_Z = moves(lambda y, q, z, x: (y, q, z + 1 - 2 * q, x))
FROM_YZ = moves(lambda y, q, z, x: (y + 1 - 2 * q, q, z + 1 - 2 * q, x))
SWAP = moves(lambda y, q, z, x: (y, 1 - q, z, x))
OUTSIDE = moves(lambda y, q, z, x: (y - 1, 1, z, x) if q == 0 else (y + 1, 0, z, x))


def send(array, pattern):
    return lax.ppermute(array, AXES, pattern)


def places_of(row_ids, shard_rows, y, q, z, x):
    group = row_ids // shard_rows
    row, column = group // NX, group % NX
    number = row // 2
    step = (2 * ((column - TILT * number) & 3) + row % 2 - (2 * x + y + 3 * z)) & 7
    after, before = ((z + 1) & 7) // 2, ((z - 1) & 7) // 2
    from_before = (step > 4) | ((step == 4) & (((number - after) & 1) == 1))
    sideways = (step >= 3) & (step <= 5)
    holder = jnp.where(sideways, jnp.where(from_before, before, after), z // 2)
    turn = (number - holder) & 3
    spot = jnp.where(turn == 0, 0, jnp.where(turn == 2, 1, jnp.where(turn == 1, 2, 3)))
    far = jnp.minimum(step, 8 - step)
    array = jnp.where(far == 2, 0, jnp.where(far == 1, 4, jnp.where(far == 3, 8, 12)))
    first = jnp.where(step == 0, 0, 4 + (from_before.astype(jnp.int32) ^ q) * 14 + array)
    return (first + spot) * shard_rows + row_ids % shard_rows


def join_kernel(count, *refs):
    piece_refs, (out_ref, sems) = refs[:count], refs[-2:]
    depth = piece_refs[0].shape[0]
    copies = [
        pltpu.make_async_copy(piece, out_ref.at[pl.ds(i * depth, depth)], sems.at[i])
        for i, piece in enumerate(piece_refs)
    ]
    for copy in copies:
        copy.start()
    for copy in copies:
        copy.wait()


def join(pieces, after):
    depth, halves, width = pieces[0].shape
    return pl.pallas_call(
        functools.partial(join_kernel, len(pieces)),
        out_shape=jax.ShapeDtypeStruct((len(pieces) * depth, halves, width), pieces[0].dtype),
        in_specs=[ANY] * (len(pieces) + len(after)),
        out_specs=ANY,
        scratch_shapes=[pltpu.SemaphoreType.DMA((len(pieces),))],
        compiler_params=pltpu.CompilerParams(vmem_limit_bytes=2**20),
        cost_estimate=pl.CostEstimate(flops=0, bytes_accessed=2 * 2**20, transcendentals=0),
    )(*pieces, *after)


def merge_kernel(core_ref, own_ref, partner_ref, both_ref, first_ref, sems):
    depth = own_ref.shape[0]
    core = core_ref[0]
    copies = [
        pltpu.make_async_copy(own_ref, both_ref.at[pl.ds(core * depth, depth)], sems.at[0]),
        pltpu.make_async_copy(partner_ref, both_ref.at[pl.ds((1 - core) * depth, depth)], sems.at[1]),
    ]
    from_own = pltpu.make_async_copy(own_ref, first_ref, sems.at[2])
    from_partner = pltpu.make_async_copy(partner_ref, first_ref, sems.at[2])
    for copy in copies:
        copy.start()

    @pl.when(core == 0)
    def _():
        from_own.start()

    @pl.when(core == 1)
    def _():
        from_partner.start()

    for copy in copies:
        copy.wait()
    from_own.wait()


def merge(core, own, partner):
    depth, halves, width = own.shape
    return pl.pallas_call(
        merge_kernel,
        out_shape=[
            jax.ShapeDtypeStruct((2 * depth, halves, width), own.dtype),
            jax.ShapeDtypeStruct(own.shape, own.dtype),
        ],
        in_specs=[SMEM, ANY, ANY],
        out_specs=[ANY, ANY],
        scratch_shapes=[pltpu.SemaphoreType.DMA((3,))],
        compiler_params=pltpu.CompilerParams(vmem_limit_bytes=2**20),
        cost_estimate=pl.CostEstimate(flops=0, bytes_accessed=3 * 2**20, transcendentals=0),
    )(core, own, partner)


def exchange_kernel(pieces, place_ref, count_ref, maps_ref, rest_ref, *refs):
    piece_refs = refs[:pieces]
    out_ref, table_ref, picked, sems = refs[pieces:]
    copies, depth = [], 0
    for i, piece in enumerate(piece_refs):
        rows = table_ref.at[pl.ds(depth, piece.shape[0])]
        copies.append(pltpu.make_async_copy(piece, rows, sems.at[i]))
        depth += piece.shape[0]
    for copy in copies:
        copy.start()
    for copy in copies:
        copy.wait()
    pairs, _, tile = maps_ref.shape
    domain = place_ref.shape[0] // pairs
    unroll = 32

    @pl.loop(0, pairs * domain // unroll)
    def _(block):
        first = pl.multiple_of(block * 2 * unroll, 2 * unroll)
        for i in range(unroll):
            row = table_ref[place_ref[block * unroll + i]]
            picked[pl.ds(first + 2 * i, 2), :] = row.astype(jnp.float32)

    rows_at = lax.broadcasted_iota(jnp.int32, (tile, tile), 0)
    columns_at = lax.broadcasted_iota(jnp.int32, (tile, tile), 1)
    together = 4

    @pl.loop(0, pairs // together)
    def _(block):
        projected = []
        for i in range(together):
            pair = block * together + i
            first = pl.multiple_of(pair * 2 * domain, 2 * domain)
            low = picked[pl.ds(first, domain, stride=2), :].astype(jnp.bfloat16)
            high = picked[pl.ds(first + 1, domain, stride=2), :].astype(jnp.bfloat16)
            rows = jnp.concatenate([low, high], axis=1)
            projected.append(
                jnp.dot(rows, maps_ref[pair], preferred_element_type=jnp.float32).astype(jnp.bfloat16)
            )
        for i in range(together):
            pair = block * together + i
            gram = lax.dot_general(
                projected[i], projected[i], (((0,), (0,)), ((), ())), preferred_element_type=jnp.float32
            )
            count = count_ref[pair]
            valid = jnp.logical_and(rows_at < count, columns_at < count)
            out_ref[pair] = jnp.where(valid, gram + rest_ref[pair], 0.0).astype(jnp.bfloat16)


def exchange(place, counts, maps, rest, pieces):
    pairs, width, tile = maps.shape
    table_rows = sum(piece.shape[0] for piece in pieces)
    return pl.pallas_call(
        functools.partial(exchange_kernel, len(pieces)),
        out_shape=jax.ShapeDtypeStruct((pairs, tile, tile), jnp.bfloat16),
        in_specs=[SMEM, SMEM, VMEM, VMEM] + [ANY] * len(pieces),
        out_specs=VMEM,
        scratch_shapes=[
            pltpu.VMEM((table_rows, 2, width // 2), jnp.bfloat16),
            pltpu.VMEM((place.shape[0] * 2, width // 2), jnp.float32),
            pltpu.SemaphoreType.DMA((len(pieces),)),
        ],
        compiler_params=pltpu.CompilerParams(vmem_limit_bytes=18 * 2**20),
        cost_estimate=pl.CostEstimate(flops=10**9, bytes_accessed=30 * 2**20, transcendentals=0),
    )(place, counts, maps, rest, *pieces)


def mask_kernel(count_ref, tiles_ref, after_ref, out_ref, tiles, sem):
    pairs, tile, _ = tiles.shape
    copy = pltpu.make_async_copy(tiles_ref, tiles, sem)
    copy.start()
    copy.wait()
    rows_at = lax.broadcasted_iota(jnp.int32, (tile, tile), 0)
    columns_at = lax.broadcasted_iota(jnp.int32, (tile, tile), 1)
    for pair in range(pairs):
        count = count_ref[pair]
        valid = jnp.logical_and(rows_at < count, columns_at < count)
        out_ref[pair] = jnp.where(valid, tiles[pair].astype(jnp.float32), 0.0).astype(jnp.bfloat16)


def mask(counts, tiles, after):
    return pl.pallas_call(
        mask_kernel,
        out_shape=jax.ShapeDtypeStruct(tiles.shape, tiles.dtype),
        in_specs=[SMEM, HBM, ANY],
        out_specs=VMEM,
        scratch_shapes=[pltpu.VMEM(tiles.shape, tiles.dtype), pltpu.SemaphoreType.DMA(())],
        compiler_params=pltpu.CompilerParams(vmem_limit_bytes=4 * 2**20),
        cost_estimate=pl.CostEstimate(flops=10**6, bytes_accessed=2**20, transcendentals=0),
    )(counts, tiles, after)


def couple_kernel(
    core_ref,
    slot_hbm,
    margin_hbm,
    coef_hbm,
    occ_hbm,
    energy_hbm,
    pool_hbm,
    outside_ref,
    own_ref,
    partner_ref,
    out_ref,
    slot_ref,
    margin_ref,
    coef_ref,
    occ_ref,
    energy_ref,
    pool_ref,
    window,
    sems,
):
    parts, pairs = slot_hbm.shape
    tile = own_ref.shape[1]
    ends = [
        (outside_ref, window.at[pl.ds(0, pairs)]),
        (own_ref, window.at[pl.ds(pairs, pairs)]),
        (partner_ref, window.at[pl.ds(2 * pairs, pairs)]),
        (pool_hbm, pool_ref),
        (slot_hbm, slot_ref),
        (margin_hbm, margin_ref),
        (coef_hbm, coef_ref),
        (occ_hbm, occ_ref),
        (energy_hbm, energy_ref),
    ]
    copies = [pltpu.make_async_copy(*end, sems.at[i]) for i, end in enumerate(ends)]
    for copy in copies:
        copy.start()
    for copy in copies:
        copy.wait()
    core = core_ref[0]
    together = 2

    @pl.loop(0, pairs // together)
    def _(block):
        halves = []
        for i in range(together):
            pair = block * together + i
            for m in range(parts):
                margin = pool_ref[margin_ref[m, pair]]
                slot = slot_ref[m, pair]
                part, rest = slot // pairs, slot % pairs
                place = jnp.where(core == 0, part, 2 - part) * pairs + rest
                half = jnp.dot(margin, window[place], preferred_element_type=jnp.float32)
                halves.append((half.astype(jnp.bfloat16), margin))
        for i in range(together):
            pair = block * together + i
            energy = jnp.broadcast_to(energy_ref[pl.ds(pair, 1), :], (tile, tile))
            shift = energy + jnp.swapaxes(energy, 0, 1) - occ_ref[pair]
            total = shift * window[pairs + pair].astype(jnp.float32)
            for m in range(parts):
                half, margin = halves[i * parts + m]
                product = lax.dot_general(
                    half, margin, (((1,), (1,)), ((), ())), preferred_element_type=jnp.float32
                )
                total += coef_ref[m, pair] * product
            out_ref[pair] = total


def couple(core, slot, margin, coef, occ, energy, pool, outside, own, partner):
    pairs, tile, _ = own.shape
    small = [slot, margin, coef, occ]
    return pl.pallas_call(
        couple_kernel,
        out_shape=jax.ShapeDtypeStruct((pairs, tile, tile), jnp.float32),
        in_specs=[SMEM] + [HBM] * 6 + [ANY] * 3,
        out_specs=VMEM,
        scratch_shapes=[pltpu.SMEM(array.shape, array.dtype) for array in small]
        + [
            pltpu.VMEM(energy.shape, energy.dtype),
            pltpu.VMEM(pool.shape, pool.dtype),
            pltpu.VMEM((3 * pairs, tile, tile), jnp.bfloat16),
            pltpu.SemaphoreType.DMA((9,)),
        ],
        compiler_params=pltpu.CompilerParams(vmem_limit_bytes=8 * 2**20),
        cost_estimate=pl.CostEstimate(flops=10**9, bytes_accessed=20 * 2**20, transcendentals=0),
    )(core, *small, energy, pool, outside, own, partner)


def per_device(
    int_table,
    dom_rows,
    pno_maps,
    amplitudes,
    pno_count,
    pno_energy,
    occ_sum,
    partner_slot,
    margin_index,
    coupling_coef,
    margin_pool,
):
    shard_rows, width = int_table.shape
    blk, grp = lax.axis_index("blk"), lax.axis_index("grp")
    y, q, z, x = blk // 2, blk % 2, grp // NX, grp % NX

    shard = int_table.reshape(shard_rows, 2, width // 2)
    masked = mask(pno_count, amplitudes, shard)
    fetched = [send(shard, pattern) for pattern in FETCHES]
    outside, partner = send(masked, OUTSIDE), send(masked, SWAP)
    place = places_of(dom_rows, shard_rows, y, q, z, x).reshape(-1)
    core = q.reshape(1)
    rest = couple(
        core,
        partner_slot.T,
        margin_index.T,
        coupling_coef.T,
        occ_sum,
        pno_energy,
        margin_pool,
        outside,
        masked,
        partner,
    )
    own = join(fetched, (rest, place))
    both, first = merge(core, own, send(own, SWAP))
    held = [send(both, FROM_X), send(both, FROM_Y), send(both, FROM_Z), send(first, FROM_YZ)]
    pieces = [both] + held + [send(part, SWAP) for part in held]
    return exchange(place, pno_count, pno_maps, rest, pieces)


def solution(mesh):
    pairs = P(AXES)
    return jax.shard_map(
        per_device,
        mesh=mesh,
        in_specs=(P("grp"),) + (pairs,) * 9 + (P("grp"),),
        out_specs=pairs,
        check_vma=False,
    )
```

time: 89.5 us -> 80.6 us (0.901)
  starting transfers between devices: 57.8 us -> 45.6 us
  waiting for transfers between devices: 11 us -> 16.4 us
  local copies, waits for them, and re-layouts: 4.99 us -> 3.14 us
  other arithmetic: 1.28 us -> 0.09 us
  Pallas kernels: 13.5 us -> 14.4 us
    ppermute x13, starting transfers between devices: 57.8 us -> 45.6 us  [send(): return lax.ppermute(array, AXES, pattern)]
    ppermute x13, waiting for transfers between devices: 11 us -> 16.4 us  [send(): return lax.ppermute(array, AXES, pattern)]
    unnamed x27 -> x23, local copies, waits for them, and re-layouts: 3.76 us -> 2.07 us
    pallas_call x0 -> x3, Pallas kernels: none -> 0.95 us  [the longest x1 0.75 us: mask(): pl.pallas_call(mask_kernel, out_shape=jax.ShapeDtypeStruct(tiles.shape, t...]
where the time goes in v2:
time: 80.6 us; the launch traced here: 79.9 us
  starting transfers between devices  45.6 us (57%)
  waiting for transfers between devices  16.4 us (20%)
  Pallas kernels  14.4 us (18%)
  local copies, waits for them, and re-layouts  3.14 us (4%)
    ppermute x13, starting transfers between devices, send(): return lax.ppermute(array, AXES, pattern)  45.6 us
    ppermute x13, waiting for transfers between devices, send(): return lax.ppermute(array, AXES, pattern)  16.4 us
    pallas_call x1, Pallas kernels, exchange(): pl.pallas_call(functools.partial(exchange_kernel, len(pieces)), out_shape...  8.22 us
    pallas_call x1, Pallas kernels, couple(): pl.pallas_call(couple_kernel, out_shape=jax.ShapeDtypeStruct((pairs, tile...  5.19 us
    unnamed x23, local copies, waits for them, and re-layouts  2.07 us
  transfers between devices with their start and end apart: 13, of which 5 were waited for; matrix products, arithmetic and copies ran while one was open for 0% of the time, Pallas kernels for 6%

profile of v2, /device:TPU:1, one launch (start us, length us, event | category | flops | bytes accessed | tf_op | source)
XLA Modules:
  0.0 79.9 jit_solution(12132723679486143737)
XLA Ops:
  0.0 1.1 %reshape.11.after_ref = bf16[512,2,128]{2,1,0:T(2,128)(2,1)S(1)} reshape(bf16[512,256]{1,0:T(8,128)(2,1)} %param.11) | data formatting | bytes 524288 | tf_op jit(solution)/shard_map/reshape | solution.py:333
  1.1 0.7 copy-done.2
  1.8 0.7 shard_map.109.own_ref
  2.5 8.8 %collective-permute-start.1 = (bf16[16,128,128]{2,1,0:T(8,128)(2,1)S(1)}, bf16[16,128,128]{2,1,0:T(8,128)(2,1)S(1)}, u32[]{:S(2)}, u32[]{:S(2)}) collective-permute-start(bf16[16,128,128]{2,1,0:T(8,128)(2,1)S(1)} %shard_map.109.own_ref), channel_id=1, source_target_pairs={{32,0},{33,1},{34,2},{35,3},{36,4},{37,5},{38,6},{39,7},{40,8},{41... | collective-permute-start | bytes 1572872 | tf_op jit(solution)/shard_map/ppermute | solution.py:49
  11.3 1.9 %collective-permute-start = (bf16[16,128,128]{2,1,0:T(8,128)(2,1)S(1)}, bf16[16,128,128]{2,1,0:T(8,128)(2,1)S(1)}, u32[]{:S(2)}, u32[]{:S(2)}) collective-permute-start(bf16[16,128,128]{2,1,0:T(8,128)(2,1)S(1)} %shard_map.109.own_ref), channel_id=1, source_target_pairs={{480,0},{481,1},{482,2},{483,3},{484,4},{485,5},{486,6},{487,7},{4... | collective-permute-start | bytes 1572872 | tf_op jit(solution)/shard_map/ppermute | solution.py:49
  13.3 2.5 %collective-permute-start.3 = (bf16[512,2,128]{2,1,0:T(2,128)(2,1)S(1)}, bf16[512,2,128]{2,1,0:T(2,128)(2,1)S(1)}, u32[]{:S(2)}, u32[]{:S(2)}) collective-permute-start(bf16[512,2,128]{2,1,0:T(2,128)(2,1)S(1)} %reshape.11.after_ref), channel_id=1, source_target_pairs={{16,0},{17,1},{18,2},{19,3},{21,4},{22,5},{23,6},{20,7},{25,8},{26... | collective-permute-start | bytes 786440 | tf_op jit(solution)/shard_map/ppermute | solution.py:49
  15.8 8.0 %collective-permute-start.2 = (bf16[512,2,128]{2,1,0:T(2,128)(2,1)S(1)}, bf16[512,2,128]{2,1,0:T(2,128)(2,1)S(1)}, u32[]{:S(2)}, u32[]{:S(2)}) collective-permute-start(bf16[512,2,128]{2,1,0:T(2,128)(2,1)S(1)} %reshape.11.after_ref), channel_id=1, source_target_pairs={{0,0},{1,1},{2,2},{3,3},{5,4},{6,5},{7,6},{4,7},{9,8},{10,9},{11,1... | collective-permute-start | bytes 786440 | tf_op jit(solution)/shard_map/ppermute | solution.py:49
  23.9 0.7 copy-done.10
  25.5 5.2 %shard_map.110.refs_2_.rest_ref = f32[16,128,128]{2,1,0:T(8,128)S(1)} custom-call(s32[1]{0:T(128)} %bitcast.core_ref, s32[6,16]{1,0:T(8,128)S(1)} %bitcast.9, s32[6,16]{1,0:T(8,128)S(1)} %bitcast.10, f32[6,16]{1,0:T(8,128)S(1)} %bitcast.11, f32[16]{0:T(128)S(1)} %copy-done.9, f32[16,128]{1,0:T(8,128)S(1)} %copy-done.5, bf16[32,128,128]{2,1,0:T(8,128)(2,1)S(1)} %copy-done.4, ...), custom_call_target="tpu_custom_call" | custom-call | flops 1000000000 | bytes 20971520 | tf_op jit(solution)/shard_map/pallas_call | solution.py:299
  30.7 5.7 %collective-permute-done.2.refs_0_ = bf16[512,2,128]{2,1,0:T(2,128)(2,1)S(1)} collective-permute-done((bf16[512,2,128]{2,1,0:T(2,128)(2,1)S(1)}, bf16[512,2,128]{2,1,0:T(2,128)(2,1)S(1)}, u32[]{:S(2)}, u32[]{:S(2)}) %collective-permute-start.2) | collective-permute-done | bytes 262176 | tf_op jit(solution)/shard_map/ppermute | solution.py:49
  36.4 2.1 %collective-permute-start.4 = (bf16[1024,2,128]{2,1,0:T(2,128)(2,1)S(1)}, bf16[1024,2,128]{2,1,0:T(2,128)(2,1)S(1)}, u32[]{:S(2)}, u32[]{:S(2)}) collective-permute-start(bf16[1024,2,128]{2,1,0:T(2,128)(2,1)S(1)} %shard_map.111.own_ref), channel_id=1, source_target_pairs={{32,0},{33,1},{34,2},{35,3},{36,4},{37,5},{38,6},{39,7},{40,8},{41... | collective-permute-start | bytes 1572872 | tf_op jit(solution)/shard_map/ppermute | solution.py:49
  38.5 1.9 %collective-permute-done.4.partner_ref = bf16[1024,2,128]{2,1,0:T(2,128)(2,1)S(1)} collective-permute-done((bf16[1024,2,128]{2,1,0:T(2,128)(2,1)S(1)}, bf16[1024,2,128]{2,1,0:T(2,128)(2,1)S(1)}, u32[]{:S(2)}, u32[]{:S(2)}) %collective-permute-start.4) | collective-permute-done | bytes 524320 | tf_op jit(solution)/shard_map/ppermute | solution.py:49
  40.5 3.0 %collective-permute-start.7 = (bf16[2048,2,128]{2,1,0:T(2,128)(2,1)S(1)}, bf16[2048,2,128]{2,1,0:T(2,128)(2,1)S(1)}, u32[]{:S(2)}, u32[]{:S(2)}) collective-permute-start(bf16[2048,2,128]{2,1,0:T(2,128)(2,1)S(1)} %get-tuple-element.7.refs_0_), channel_id=1, source_target_pairs={{4,0},{5,1},{6,2},{7,3},{8,4},{9,5},{10,6},{11,7},{12,8},{13,9},{1... | collective-permute-start | bytes 3145736 | tf_op jit(solution)/shard_map/ppermute | solution.py:49
  43.6 1.9 %collective-permute-start.6 = (bf16[2048,2,128]{2,1,0:T(2,128)(2,1)S(1)}, bf16[2048,2,128]{2,1,0:T(2,128)(2,1)S(1)}, u32[]{:S(2)}, u32[]{:S(2)}) collective-permute-start(bf16[2048,2,128]{2,1,0:T(2,128)(2,1)S(1)} %get-tuple-element.7.refs_0_), channel_id=1, source_target_pairs={{64,0},{65,1},{66,2},{67,3},{68,4},{69,5},{70,6},{71,7},{72,8},{73... | collective-permute-start | bytes 3145736 | tf_op jit(solution)/shard_map/ppermute | solution.py:49
  45.5 2.1 %collective-permute-start.5 = (bf16[2048,2,128]{2,1,0:T(2,128)(2,1)S(1)}, bf16[2048,2,128]{2,1,0:T(2,128)(2,1)S(1)}, u32[]{:S(2)}, u32[]{:S(2)}) collective-permute-start(bf16[2048,2,128]{2,1,0:T(2,128)(2,1)S(1)} %get-tuple-element.7.refs_0_), channel_id=1, source_target_pairs={{1,0},{2,1},{3,2},{0,3},{5,4},{6,5},{7,6},{4,7},{9,8},{10,9},{11,1... | collective-permute-start | bytes 3145736 | tf_op jit(solution)/shard_map/ppermute | solution.py:49
  47.6 3.5 %collective-permute-start.8 = (bf16[1024,2,128]{2,1,0:T(2,128)(2,1)S(1)}, bf16[1024,2,128]{2,1,0:T(2,128)(2,1)S(1)}, u32[]{:S(2)}, u32[]{:S(2)}) collective-permute-start(bf16[1024,2,128]{2,1,0:T(2,128)(2,1)S(1)} %get-tuple-element.8), channel_id=1, source_target_pairs={{68,0},{69,1},{70,2},{71,3},{72,4},{73,5},{74,6},{75,7},{76,8},{77... | collective-permute-start | bytes 1572872 | tf_op jit(solution)/shard_map/ppermute | solution.py:49
  51.1 6.1 %collective-permute-done.7.refs_3_ = bf16[2048,2,128]{2,1,0:T(2,128)(2,1)S(1)} collective-permute-done((bf16[2048,2,128]{2,1,0:T(2,128)(2,1)S(1)}, bf16[2048,2,128]{2,1,0:T(2,128)(2,1)S(1)}, u32[]{:S(2)}, u32[]{:S(2)}) %collective-permute-start.7) | collective-permute-done | bytes 1048608 | tf_op jit(solution)/shard_map/ppermute | solution.py:49
  57.3 2.4 %collective-permute-start.11 = (bf16[2048,2,128]{2,1,0:T(2,128)(2,1)S(1)}, bf16[2048,2,128]{2,1,0:T(2,128)(2,1)S(1)}, u32[]{:S(2)}, u32[]{:S(2)}) collective-permute-start(bf16[2048,2,128]{2,1,0:T(2,128)(2,1)S(1)} %collective-permute-done.7.refs_3_), channel_id=1, source_target_pairs={{32,0},{33,1},{34,2},{35,3},{36,4},{37,5},{38,6},{39,7},{40,8},{41... | collective-permute-start | bytes 3145736 | tf_op jit(solution)/shard_map/ppermute | solution.py:49
  59.7 0.8 collective-permute-done.6.refs_2_
  60.5 3.2 %collective-permute-start.10 = (bf16[2048,2,128]{2,1,0:T(2,128)(2,1)S(1)}, bf16[2048,2,128]{2,1,0:T(2,128)(2,1)S(1)}, u32[]{:S(2)}, u32[]{:S(2)}) collective-permute-start(bf16[2048,2,128]{2,1,0:T(2,128)(2,1)S(1)} %collective-permute-done.6.refs_2_), channel_id=1, source_target_pairs={{32,0},{33,1},{34,2},{35,3},{36,4},{37,5},{38,6},{39,7},{40,8},{41... | collective-permute-start | bytes 3145736 | tf_op jit(solution)/shard_map/ppermute | solution.py:49
  63.7 4.1 %collective-permute-start.9 = (bf16[2048,2,128]{2,1,0:T(2,128)(2,1)S(1)}, bf16[2048,2,128]{2,1,0:T(2,128)(2,1)S(1)}, u32[]{:S(2)}, u32[]{:S(2)}) collective-permute-start(bf16[2048,2,128]{2,1,0:T(2,128)(2,1)S(1)} %collective-permute-done.5.refs_1_), channel_id=1, source_target_pairs={{32,0},{33,1},{34,2},{35,3},{36,4},{37,5},{38,6},{39,7},{40,8},{41... | collective-permute-start | bytes 3145736 | tf_op jit(solution)/shard_map/ppermute | solution.py:49
  67.8 1.9 %collective-permute-start.12 = (bf16[1024,2,128]{2,1,0:T(2,128)(2,1)S(1)}, bf16[1024,2,128]{2,1,0:T(2,128)(2,1)S(1)}, u32[]{:S(2)}, u32[]{:S(2)}) collective-permute-start(bf16[1024,2,128]{2,1,0:T(2,128)(2,1)S(1)} %collective-permute-done.8.refs_4_), channel_id=1, source_target_pairs={{32,0},{33,1},{34,2},{35,3},{36,4},{37,5},{38,6},{39,7},{40,8},{41... | collective-permute-start | bytes 1572872 | tf_op jit(solution)/shard_map/ppermute | solution.py:49
  69.8 1.9 %collective-permute-done.12.refs_8_ = bf16[1024,2,128]{2,1,0:T(2,128)(2,1)S(1)} collective-permute-done((bf16[1024,2,128]{2,1,0:T(2,128)(2,1)S(1)}, bf16[1024,2,128]{2,1,0:T(2,128)(2,1)S(1)}, u32[]{:S(2)}, u32[]{:S(2)}) %collective-permute-start.12) | collective-permute-done | bytes 524320 | tf_op jit(solution)/shard_map/ppermute | solution.py:49
  71.7 8.2 %shard_map.113 = bf16[16,128,128]{2,1,0:T(8,128)(2,1)} custom-call(s32[4096]{0:T(1024)S(1)} %bitcast.8, s32[16]{0:T(128)S(1)} %copy-done.3, bf16[16,256,128]{2,1,0:T(8,128)(2,1)S(1)} %copy-done, f32[16,128,128]{2,1,0:T(8,128)S(1)} %shard_map.110.refs_2_.rest_ref, bf16[2048,2,128]{2,1,0:T(2,128)(2,1)S(1)} %get-tuple-element.7.refs_0_, ...), custom_call_target="tpu_custom_call" | custom-call | flops 1000000000 | bytes 31457280 | tf_op jit(solution)/shard_map/pallas_call | solution.py:188
  (32 shorter events, 1.0 us)
Async XLA Ops:
  0.0 1.1 %copy-start.1 = (bf16[16,128,128]{2,1,0:T(8,128)(2,1)S(1)}, bf16[16,128,128]{2,1,0:T(8,128)(2,1)}, u32[]{:S(2)}) copy-start(bf16[16,128,128]{2,1,0:T(8,128)(2,1)} %tiles_ref.1) | copy-start | bytes 1572868
  1.1 0.7 copy-start.2
  1.8 23.0 %copy-start.4 = (bf16[32,128,128]{2,1,0:T(8,128)(2,1)S(1)}, bf16[32,128,128]{2,1,0:T(8,128)(2,1)}, u32[]{:S(2)}) copy-start(bf16[32,128,128]{2,1,0:T(8,128)(2,1)} %pool_hbm.1) | copy-start | bytes 3145732
  2.5 22.2 %collective-permute-start.1 = (bf16[16,128,128]{2,1,0:T(8,128)(2,1)S(1)}, bf16[16,128,128]{2,1,0:T(8,128)(2,1)S(1)}, u32[]{:S(2)}, u32[]{:S(2)}) collective-permute-start(bf16[16,128,128]{2,1,0:T(8,128)(2,1)S(1)} %shard_map.109.own_ref), channel_id=1, source_target_pairs={{32,0},{33,1},{34,2},{35,3},{36,4},{37,5},{38,6},{39,7},{40,8},{41... | collective-permute-start | bytes 1572872 | tf_op jit(solution)/shard_map/ppermute | solution.py:49
  11.3 13.5 %collective-permute-start = (bf16[16,128,128]{2,1,0:T(8,128)(2,1)S(1)}, bf16[16,128,128]{2,1,0:T(8,128)(2,1)S(1)}, u32[]{:S(2)}, u32[]{:S(2)}) collective-permute-start(bf16[16,128,128]{2,1,0:T(8,128)(2,1)S(1)} %shard_map.109.own_ref), channel_id=1, source_target_pairs={{480,0},{481,1},{482,2},{483,3},{484,4},{485,5},{486,6},{487,7},{4... | collective-permute-start | bytes 1572872 | tf_op jit(solution)/shard_map/ppermute | solution.py:49
  13.3 17.4 %collective-permute-start.3 = (bf16[512,2,128]{2,1,0:T(2,128)(2,1)S(1)}, bf16[512,2,128]{2,1,0:T(2,128)(2,1)S(1)}, u32[]{:S(2)}, u32[]{:S(2)}) collective-permute-start(bf16[512,2,128]{2,1,0:T(2,128)(2,1)S(1)} %reshape.11.after_ref), channel_id=1, source_target_pairs={{16,0},{17,1},{18,2},{19,3},{21,4},{22,5},{23,6},{20,7},{25,8},{26... | collective-permute-start | bytes 786440 | tf_op jit(solution)/shard_map/ppermute | solution.py:49
  15.8 20.5 %collective-permute-start.2 = (bf16[512,2,128]{2,1,0:T(2,128)(2,1)S(1)}, bf16[512,2,128]{2,1,0:T(2,128)(2,1)S(1)}, u32[]{:S(2)}, u32[]{:S(2)}) collective-permute-start(bf16[512,2,128]{2,1,0:T(2,128)(2,1)S(1)} %reshape.11.after_ref), channel_id=1, source_target_pairs={{0,0},{1,1},{2,2},{3,3},{5,4},{6,5},{7,6},{4,7},{9,8},{10,9},{11,1... | collective-permute-start | bytes 786440 | tf_op jit(solution)/shard_map/ppermute | solution.py:49
  23.9 0.7 copy-start.10
  24.7 0.7 copy-start.5
  24.7 0.7 copy-start.7
  24.7 0.7 copy-start.8
  24.8 0.7 copy-start.6
  24.8 0.7 copy-start.9
  36.4 35.3 %copy-start = (bf16[16,256,128]{2,1,0:T(8,128)(2,1)S(1)}, bf16[16,256,128]{2,1,0:T(8,128)(2,1)}, u32[]{:S(2)}) copy-start(bf16[16,256,128]{2,1,0:T(8,128)(2,1)} %maps_ref.1) | copy-start | bytes 3145732
  36.4 3.9 %collective-permute-start.4 = (bf16[1024,2,128]{2,1,0:T(2,128)(2,1)S(1)}, bf16[1024,2,128]{2,1,0:T(2,128)(2,1)S(1)}, u32[]{:S(2)}, u32[]{:S(2)}) collective-permute-start(bf16[1024,2,128]{2,1,0:T(2,128)(2,1)S(1)} %shard_map.111.own_ref), channel_id=1, source_target_pairs={{32,0},{33,1},{34,2},{35,3},{36,4},{37,5},{38,6},{39,7},{40,8},{41... | collective-permute-start | bytes 1572872 | tf_op jit(solution)/shard_map/ppermute | solution.py:49
  40.5 31.2 %copy-start.3 = (s32[16]{0:T(128)S(1)}, s32[16]{0:T(128)}, u32[]{:S(2)}) copy-start(s32[16]{0:T(128)} %count_ref.3) | copy-start | bytes 196
  40.5 16.8 %collective-permute-start.7 = (bf16[2048,2,128]{2,1,0:T(2,128)(2,1)S(1)}, bf16[2048,2,128]{2,1,0:T(2,128)(2,1)S(1)}, u32[]{:S(2)}, u32[]{:S(2)}) collective-permute-start(bf16[2048,2,128]{2,1,0:T(2,128)(2,1)S(1)} %get-tuple-element.7.refs_0_), channel_id=1, source_target_pairs={{4,0},{5,1},{6,2},{7,3},{8,4},{9,5},{10,6},{11,7},{12,8},{13,9},{1... | collective-permute-start | bytes 3145736 | tf_op jit(solution)/shard_map/ppermute | solution.py:49
  43.6 16.9 %collective-permute-start.6 = (bf16[2048,2,128]{2,1,0:T(2,128)(2,1)S(1)}, bf16[2048,2,128]{2,1,0:T(2,128)(2,1)S(1)}, u32[]{:S(2)}, u32[]{:S(2)}) collective-permute-start(bf16[2048,2,128]{2,1,0:T(2,128)(2,1)S(1)} %get-tuple-element.7.refs_0_), channel_id=1, source_target_pairs={{64,0},{65,1},{66,2},{67,3},{68,4},{69,5},{70,6},{71,7},{72,8},{73... | collective-permute-start | bytes 3145736 | tf_op jit(solution)/shard_map/ppermute | solution.py:49
  45.5 18.2 %collective-permute-start.5 = (bf16[2048,2,128]{2,1,0:T(2,128)(2,1)S(1)}, bf16[2048,2,128]{2,1,0:T(2,128)(2,1)S(1)}, u32[]{:S(2)}, u32[]{:S(2)}) collective-permute-start(bf16[2048,2,128]{2,1,0:T(2,128)(2,1)S(1)} %get-tuple-element.7.refs_0_), channel_id=1, source_target_pairs={{1,0},{2,1},{3,2},{0,3},{5,4},{6,5},{7,6},{4,7},{9,8},{10,9},{11,1... | collective-permute-start | bytes 3145736 | tf_op jit(solution)/shard_map/ppermute | solution.py:49
  47.6 20.2 %collective-permute-start.8 = (bf16[1024,2,128]{2,1,0:T(2,128)(2,1)S(1)}, bf16[1024,2,128]{2,1,0:T(2,128)(2,1)S(1)}, u32[]{:S(2)}, u32[]{:S(2)}) collective-permute-start(bf16[1024,2,128]{2,1,0:T(2,128)(2,1)S(1)} %get-tuple-element.8), channel_id=1, source_target_pairs={{68,0},{69,1},{70,2},{71,3},{72,4},{73,5},{74,6},{75,7},{76,8},{77... | collective-permute-start | bytes 1572872 | tf_op jit(solution)/shard_map/ppermute | solution.py:49
  57.3 14.4 %collective-permute-start.11 = (bf16[2048,2,128]{2,1,0:T(2,128)(2,1)S(1)}, bf16[2048,2,128]{2,1,0:T(2,128)(2,1)S(1)}, u32[]{:S(2)}, u32[]{:S(2)}) collective-permute-start(bf16[2048,2,128]{2,1,0:T(2,128)(2,1)S(1)} %collective-permute-done.7.refs_3_), channel_id=1, source_target_pairs={{32,0},{33,1},{34,2},{35,3},{36,4},{37,5},{38,6},{39,7},{40,8},{41... | collective-permute-start | bytes 3145736 | tf_op jit(solution)/shard_map/ppermute | solution.py:49
  60.5 11.2 %collective-permute-start.10 = (bf16[2048,2,128]{2,1,0:T(2,128)(2,1)S(1)}, bf16[2048,2,128]{2,1,0:T(2,128)(2,1)S(1)}, u32[]{:S(2)}, u32[]{:S(2)}) collective-permute-start(bf16[2048,2,128]{2,1,0:T(2,128)(2,1)S(1)} %collective-permute-done.6.refs_2_), channel_id=1, source_target_pairs={{32,0},{33,1},{34,2},{35,3},{36,4},{37,5},{38,6},{39,7},{40,8},{41... | collective-permute-start | bytes 3145736 | tf_op jit(solution)/shard_map/ppermute | solution.py:49
  63.7 8.0 %collective-permute-start.9 = (bf16[2048,2,128]{2,1,0:T(2,128)(2,1)S(1)}, bf16[2048,2,128]{2,1,0:T(2,128)(2,1)S(1)}, u32[]{:S(2)}, u32[]{:S(2)}) collective-permute-start(bf16[2048,2,128]{2,1,0:T(2,128)(2,1)S(1)} %collective-permute-done.5.refs_1_), channel_id=1, source_target_pairs={{32,0},{33,1},{34,2},{35,3},{36,4},{37,5},{38,6},{39,7},{40,8},{41... | collective-permute-start | bytes 3145736 | tf_op jit(solution)/shard_map/ppermute | solution.py:49
  67.8 3.8 %collective-permute-start.12 = (bf16[1024,2,128]{2,1,0:T(2,128)(2,1)S(1)}, bf16[1024,2,128]{2,1,0:T(2,128)(2,1)S(1)}, u32[]{:S(2)}, u32[]{:S(2)}) collective-permute-start(bf16[1024,2,128]{2,1,0:T(2,128)(2,1)S(1)} %collective-permute-done.8.refs_4_), channel_id=1, source_target_pairs={{32,0},{33,1},{34,2},{35,3},{36,4},{37,5},{38,6},{39,7},{40,8},{41... | collective-permute-start | bytes 1572872 | tf_op jit(solution)/shard_map/ppermute | solution.py:49

commit v3 on v2

--- a/solution.py
+++ b/solution.py
@@ -92,7 +92,23 @@
     )(*pieces, *after)
 
 
-def merge_kernel(core_ref, own_ref, partner_ref, both_ref, first_ref, sems):
+def once_kernel(array_ref, after_ref, out_ref):
+    pass
+
+
+def once(array, after):
+    return pl.pallas_call(
+        once_kernel,
+        out_shape=jax.ShapeDtypeStruct(array.shape, array.dtype),
+        in_specs=[ANY, ANY],
+        out_specs=ANY,
+        input_output_aliases={0: 0},
+        compiler_params=pltpu.CompilerParams(vmem_limit_bytes=2**20),
+    )(array, after)
+
+
+def merge_kernel(core_ref, own_ref, partner_ref, *refs):
+    both_ref, first_ref, sems = refs[-3:]
     depth = own_ref.shape[0]
     core = core_ref[0]
     copies = [
@@ -117,7 +133,7 @@
     from_own.wait()
 
 
-def merge(core, own, partner):
+def merge(core, own, partner, after):
     depth, halves, width = own.shape
     return pl.pallas_call(
         merge_kernel,
@@ -125,12 +141,12 @@
             jax.ShapeDtypeStruct((2 * depth, halves, width), own.dtype),
             jax.ShapeDtypeStruct(own.shape, own.dtype),
         ],
-        in_specs=[SMEM, ANY, ANY],
+        in_specs=[SMEM, ANY, ANY] + [ANY] * len(after),
         out_specs=[ANY, ANY],
         scratch_shapes=[pltpu.SemaphoreType.DMA((3,))],
         compiler_params=pltpu.CompilerParams(vmem_limit_bytes=2**20),
         cost_estimate=pl.CostEstimate(flops=0, bytes_accessed=3 * 2**20, transcendentals=0),
-    )(core, own, partner)
+    )(core, own, partner, *after)
 
 
 def exchange_kernel(pieces, place_ref, count_ref, maps_ref, rest_ref, *refs):
@@ -147,7 +163,7 @@
         copy.wait()
     pairs, _, tile = maps_ref.shape
     domain = place_ref.shape[0] // pairs
-    unroll = 32
+    unroll = 128
 
     @pl.loop(0, pairs * domain // unroll)
     def _(block):
@@ -158,28 +174,20 @@
 
     rows_at = lax.broadcasted_iota(jnp.int32, (tile, tile), 0)
     columns_at = lax.broadcasted_iota(jnp.int32, (tile, tile), 1)
-    together = 4
-
-    @pl.loop(0, pairs // together)
-    def _(block):
-        projected = []
-        for i in range(together):
-            pair = block * together + i
-            first = pl.multiple_of(pair * 2 * domain, 2 * domain)
-            low = picked[pl.ds(first, domain, stride=2), :].astype(jnp.bfloat16)
-            high = picked[pl.ds(first + 1, domain, stride=2), :].astype(jnp.bfloat16)
-            rows = jnp.concatenate([low, high], axis=1)
-            projected.append(
-                jnp.dot(rows, maps_ref[pair], preferred_element_type=jnp.float32).astype(jnp.bfloat16)
-            )
-        for i in range(together):
-            pair = block * together + i
-            gram = lax.dot_general(
-                projected[i], projected[i], (((0,), (0,)), ((), ())), preferred_element_type=jnp.float32
-            )
-            count = count_ref[pair]
-            valid = jnp.logical_and(rows_at < count, columns_at < count)
-            out_ref[pair] = jnp.where(valid, gram + rest_ref[pair], 0.0).astype(jnp.bfloat16)
+    projected = []
+    for pair in range(pairs):
+        first = pair * 2 * domain
+        low = picked[pl.ds(first, domain, stride=2), :].astype(jnp.bfloat16)
+        high = picked[pl.ds(first + 1, domain, stride=2), :].astype(jnp.bfloat16)
+        rows = jnp.concatenate([low, high], axis=1)
+        projected.append(jnp.dot(rows, maps_ref[pair], preferred_element_type=jnp.float32).astype(jnp.bfloat16))
+    for pair in range(pairs):
+        gram = lax.dot_general(
+            projected[pair], projected[pair], (((0,), (0,)), ((), ())), preferred_element_type=jnp.float32
+        )
+        count = count_ref[pair]
+        valid = jnp.logical_and(rows_at < count, columns_at < count)
+        out_ref[pair] = jnp.where(valid, gram + rest_ref[pair], 0.0).astype(jnp.bfloat16)
 
 
 def exchange(place, counts, maps, rest, pieces):
@@ -195,7 +203,7 @@
             pltpu.VMEM((place.shape[0] * 2, width // 2), jnp.float32),
             pltpu.SemaphoreType.DMA((len(pieces),)),
         ],
-        compiler_params=pltpu.CompilerParams(vmem_limit_bytes=18 * 2**20),
+        compiler_params=pltpu.CompilerParams(vmem_limit_bytes=24 * 2**20),
         cost_estimate=pl.CostEstimate(flops=10**9, bytes_accessed=30 * 2**20, transcendentals=0),
     )(place, counts, maps, rest, *pieces)
 
@@ -236,6 +244,7 @@
     outside_ref,
     own_ref,
     partner_ref,
+    after_ref,
     out_ref,
     slot_ref,
     margin_ref,
@@ -265,7 +274,7 @@
     for copy in copies:
         copy.wait()
     core = core_ref[0]
-    together = 2
+    together = 8
 
     @pl.loop(0, pairs // together)
     def _(block):
@@ -293,13 +302,13 @@
             out_ref[pair] = total
 
 
-def couple(core, slot, margin, coef, occ, energy, pool, outside, own, partner):
+def couple(core, slot, margin, coef, occ, energy, pool, outside, own, partner, after):
     pairs, tile, _ = own.shape
     small = [slot, margin, coef, occ]
     return pl.pallas_call(
         couple_kernel,
         out_shape=jax.ShapeDtypeStruct((pairs, tile, tile), jnp.float32),
-        in_specs=[SMEM] + [HBM] * 6 + [ANY] * 3,
+        in_specs=[SMEM] + [HBM] * 6 + [ANY] * 4,
         out_specs=VMEM,
         scratch_shapes=[pltpu.SMEM(array.shape, array.dtype) for array in small]
         + [
@@ -308,9 +317,9 @@
             pltpu.VMEM((3 * pairs, tile, tile), jnp.bfloat16),
             pltpu.SemaphoreType.DMA((9,)),
         ],
-        compiler_params=pltpu.CompilerParams(vmem_limit_bytes=8 * 2**20),
+        compiler_params=pltpu.CompilerParams(vmem_limit_bytes=16 * 2**20),
         cost_estimate=pl.CostEstimate(flops=10**9, bytes_accessed=20 * 2**20, transcendentals=0),
-    )(core, *small, energy, pool, outside, own, partner)
+    )(core, *small, energy, pool, outside, own, partner, after)
 
 
 def per_device(
@@ -336,6 +345,9 @@
     outside, partner = send(masked, OUTSIDE), send(masked, SWAP)
     place = places_of(dom_rows, shard_rows, y, q, z, x).reshape(-1)
     core = q.reshape(1)
+    own = join(fetched, (place,))
+    both, first = merge(core, own, send(own, SWAP), (outside, partner))
+    held = [send(both, FROM_X), send(both, FROM_Y), send(both, FROM_Z), send(first, FROM_YZ)]
     rest = couple(
         core,
         partner_slot.T,
@@ -347,10 +359,9 @@
         outside,
         masked,
         partner,
+        both,
     )
-    own = join(fetched, (rest, place))
-    both, first = merge(core, own, send(own, SWAP))
-    held = [send(both, FROM_X), send(both, FROM_Y), send(both, FROM_Z), send(first, FROM_YZ)]
+    held = [once(part, rest) for part in held]
     pieces = [both] + held + [send(part, SWAP) for part in held]
     return exchange(place, pno_count, pno_maps, rest, pieces)
 

time: 80.6 us -> 73.4 us (0.911)
  waiting for transfers between devices: 16.4 us -> 7.61 us
  starting transfers between devices: 45.6 us -> 49.9 us
  Pallas kernels: 14.4 us -> 11.7 us
    ppermute x13, waiting for transfers between devices: 16.4 us -> 7.61 us  [send(): return lax.ppermute(array, AXES, pattern)]
    ppermute x13, starting transfers between devices: 45.6 us -> 49.9 us  [send(): return lax.ppermute(array, AXES, pattern)]
    pallas_call x1, Pallas kernels: 8.22 us -> 6.63 us  [exchange(): pl.pallas_call(functools.partial(exchange_kernel, len(pieces)), out_shape...]
    pallas_call x1, Pallas kernels: 5.19 us -> 4.15 us  [couple(): pl.pallas_call(couple_kernel, out_shape=jax.ShapeDtypeStruct((pairs, tile...]
  transfers between devices with their start and end apart: 13 -> 13, of which waited for: 5 -> 6; matrix products, arithmetic and copies ran while one was open for 0% -> 0% of each run, Pallas kernels for 6% -> 7%
where the time goes in v3:
time: 73.4 us; the launch traced here: 72.8 us
  starting transfers between devices  49.9 us (68%)
  Pallas kernels  11.7 us (16%)
  waiting for transfers between devices  7.61 us (10%)
  local copies, waits for them, and re-layouts  3.06 us (4%)
    ppermute x13, starting transfers between devices, send(): return lax.ppermute(array, AXES, pattern)  49.9 us
    ppermute x13, waiting for transfers between devices, send(): return lax.ppermute(array, AXES, pattern)  7.61 us
    pallas_call x1, Pallas kernels, exchange(): pl.pallas_call(functools.partial(exchange_kernel, len(pieces)), out_shape...  6.63 us
    pallas_call x1, Pallas kernels, couple(): pl.pallas_call(couple_kernel, out_shape=jax.ShapeDtypeStruct((pairs, tile...  4.15 us
    unnamed x23, local copies, waits for them, and re-layouts  1.99 us
  transfers between devices with their start and end apart: 13, of which 6 were waited for; matrix products, arithmetic and copies ran while one was open for 0% of the time, Pallas kernels for 7%

profile of v3, /device:TPU:1, one launch (start us, length us, event | category | flops | bytes accessed | tf_op | source)
XLA Modules:
  0.0 72.8 jit_solution(18118467704475711985)
XLA Ops:
  0.0 1.1 %reshape.11.after_ref = bf16[512,2,128]{2,1,0:T(2,128)(2,1)S(1)} reshape(bf16[512,256]{1,0:T(8,128)(2,1)} %param.11) | data formatting | bytes 524288 | tf_op jit(solution)/shard_map/reshape | solution.py:342
  1.1 7.6 %collective-permute-start.3 = (bf16[512,2,128]{2,1,0:T(2,128)(2,1)S(1)}, bf16[512,2,128]{2,1,0:T(2,128)(2,1)S(1)}, u32[]{:S(2)}, u32[]{:S(2)}) collective-permute-start(bf16[512,2,128]{2,1,0:T(2,128)(2,1)S(1)} %reshape.11.after_ref), channel_id=1, source_target_pairs={{16,0},{17,1},{18,2},{19,3},{21,4},{22,5},{23,6},{20,7},{25,8},{26... | collective-permute-start | bytes 786440 | tf_op jit(solution)/shard_map/ppermute | solution.py:49
  8.7 8.0 %collective-permute-start.2 = (bf16[512,2,128]{2,1,0:T(2,128)(2,1)S(1)}, bf16[512,2,128]{2,1,0:T(2,128)(2,1)S(1)}, u32[]{:S(2)}, u32[]{:S(2)}) collective-permute-start(bf16[512,2,128]{2,1,0:T(2,128)(2,1)S(1)} %reshape.11.after_ref), channel_id=1, source_target_pairs={{0,0},{1,1},{2,2},{3,3},{5,4},{6,5},{7,6},{4,7},{9,8},{10,9},{11,1... | collective-permute-start | bytes 786440 | tf_op jit(solution)/shard_map/ppermute | solution.py:49
  17.4 0.7 %shard_map.109.own_ref = bf16[16,128,128]{2,1,0:T(8,128)(2,1)S(1)} custom-call(s32[16]{0:T(128)S(1)} %copy-done.7, bf16[16,128,128]{2,1,0:T(8,128)(2,1)S(1)} %copy-done.2, bf16[512,2,128]{2,1,0:T(2,128)(2,1)S(1)} %reshape.11.after_ref), custom_call_target="tpu_custom_call" | custom-call | flops 1000000 | bytes 1048576 | tf_op jit(solution)/shard_map/pallas_call | solution.py:225
  18.1 1.9 %collective-permute-start.1 = (bf16[16,128,128]{2,1,0:T(8,128)(2,1)S(1)}, bf16[16,128,128]{2,1,0:T(8,128)(2,1)S(1)}, u32[]{:S(2)}, u32[]{:S(2)}) collective-permute-start(bf16[16,128,128]{2,1,0:T(8,128)(2,1)S(1)} %shard_map.109.own_ref), channel_id=1, source_target_pairs={{32,0},{33,1},{34,2},{35,3},{36,4},{37,5},{38,6},{39,7},{40,8},{41... | collective-permute-start | bytes 1572872 | tf_op jit(solution)/shard_map/ppermute | solution.py:49
  20.1 4.8 %collective-permute-start = (bf16[16,128,128]{2,1,0:T(8,128)(2,1)S(1)}, bf16[16,128,128]{2,1,0:T(8,128)(2,1)S(1)}, u32[]{:S(2)}, u32[]{:S(2)}) collective-permute-start(bf16[16,128,128]{2,1,0:T(8,128)(2,1)S(1)} %shard_map.109.own_ref), channel_id=1, source_target_pairs={{480,0},{481,1},{482,2},{483,3},{484,4},{485,5},{486,6},{487,7},{4... | collective-permute-start | bytes 1572872 | tf_op jit(solution)/shard_map/ppermute | solution.py:49
  24.9 0.7 copy-done.10
  25.7 0.8 %collective-permute-done.3.refs_1_ = bf16[512,2,128]{2,1,0:T(2,128)(2,1)S(1)} collective-permute-done((bf16[512,2,128]{2,1,0:T(2,128)(2,1)S(1)}, bf16[512,2,128]{2,1,0:T(2,128)(2,1)S(1)}, u32[]{:S(2)}, u32[]{:S(2)}) %collective-permute-start.3) | collective-permute-done | bytes 262176 | tf_op jit(solution)/shard_map/ppermute | solution.py:49
  26.5 2.4 %collective-permute-done.2.refs_0_ = bf16[512,2,128]{2,1,0:T(2,128)(2,1)S(1)} collective-permute-done((bf16[512,2,128]{2,1,0:T(2,128)(2,1)S(1)}, bf16[512,2,128]{2,1,0:T(2,128)(2,1)S(1)}, u32[]{:S(2)}, u32[]{:S(2)}) %collective-permute-start.2) | collective-permute-done | bytes 262176 | tf_op jit(solution)/shard_map/ppermute | solution.py:49
  28.9 1.9 %collective-permute-start.4 = (bf16[1024,2,128]{2,1,0:T(2,128)(2,1)S(1)}, bf16[1024,2,128]{2,1,0:T(2,128)(2,1)S(1)}, u32[]{:S(2)}, u32[]{:S(2)}) collective-permute-start(bf16[1024,2,128]{2,1,0:T(2,128)(2,1)S(1)} %shard_map.110.own_ref), channel_id=1, source_target_pairs={{32,0},{33,1},{34,2},{35,3},{36,4},{37,5},{38,6},{39,7},{40,8},{41... | collective-permute-start | bytes 1572872 | tf_op jit(solution)/shard_map/ppermute | solution.py:49
  30.9 1.1 %collective-permute-done.refs_0_.outside_ref = bf16[16,128,128]{2,1,0:T(8,128)(2,1)S(1)} collective-permute-done((bf16[16,128,128]{2,1,0:T(8,128)(2,1)S(1)}, bf16[16,128,128]{2,1,0:T(8,128)(2,1)S(1)}, u32[]{:S(2)}, u32[]{:S(2)}) %collective-permute-start) | collective-permute-done | bytes 524320 | tf_op jit(solution)/shard_map/ppermute | solution.py:49
  32.0 0.8 %collective-permute-done.4.partner_ref = bf16[1024,2,128]{2,1,0:T(2,128)(2,1)S(1)} collective-permute-done((bf16[1024,2,128]{2,1,0:T(2,128)(2,1)S(1)}, bf16[1024,2,128]{2,1,0:T(2,128)(2,1)S(1)}, u32[]{:S(2)}, u32[]{:S(2)}) %collective-permute-start.4) | collective-permute-done | bytes 524320 | tf_op jit(solution)/shard_map/ppermute | solution.py:49
  32.9 2.7 %collective-permute-start.7 = (bf16[2048,2,128]{2,1,0:T(2,128)(2,1)S(1)}, bf16[2048,2,128]{2,1,0:T(2,128)(2,1)S(1)}, u32[]{:S(2)}, u32[]{:S(2)}) collective-permute-start(bf16[2048,2,128]{2,1,0:T(2,128)(2,1)S(1)} %get-tuple-element.7.after_ref.refs_0_), channel_id=1, source_target_pairs={{4,0},{5,1},{6,2},{7,3},{8,4},{9,5},{10,6},{11,7},{12,8},{13,9},{1... | collective-permute-start | bytes 3145736 | tf_op jit(solution)/shard_map/ppermute | solution.py:49
  35.7 3.3 %collective-permute-start.6 = (bf16[2048,2,128]{2,1,0:T(2,128)(2,1)S(1)}, bf16[2048,2,128]{2,1,0:T(2,128)(2,1)S(1)}, u32[]{:S(2)}, u32[]{:S(2)}) collective-permute-start(bf16[2048,2,128]{2,1,0:T(2,128)(2,1)S(1)} %get-tuple-element.7.after_ref.refs_0_), channel_id=1, source_target_pairs={{64,0},{65,1},{66,2},{67,3},{68,4},{69,5},{70,6},{71,7},{72,8},{73... | collective-permute-start | bytes 3145736 | tf_op jit(solution)/shard_map/ppermute | solution.py:49
  38.9 1.9 %collective-permute-start.5 = (bf16[2048,2,128]{2,1,0:T(2,128)(2,1)S(1)}, bf16[2048,2,128]{2,1,0:T(2,128)(2,1)S(1)}, u32[]{:S(2)}, u32[]{:S(2)}) collective-permute-start(bf16[2048,2,128]{2,1,0:T(2,128)(2,1)S(1)} %get-tuple-element.7.after_ref.refs_0_), channel_id=1, source_target_pairs={{1,0},{2,1},{3,2},{0,3},{5,4},{6,5},{7,6},{4,7},{9,8},{10,9},{11,1... | collective-permute-start | bytes 3145736 | tf_op jit(solution)/shard_map/ppermute | solution.py:49
  40.9 4.4 %collective-permute-start.8 = (bf16[1024,2,128]{2,1,0:T(2,128)(2,1)S(1)}, bf16[1024,2,128]{2,1,0:T(2,128)(2,1)S(1)}, u32[]{:S(2)}, u32[]{:S(2)}) collective-permute-start(bf16[1024,2,128]{2,1,0:T(2,128)(2,1)S(1)} %get-tuple-element.8), channel_id=1, source_target_pairs={{68,0},{69,1},{70,2},{71,3},{72,4},{73,5},{74,6},{75,7},{76,8},{77... | collective-permute-start | bytes 1572872 | tf_op jit(solution)/shard_map/ppermute | solution.py:49
  46.0 4.1 %shard_map.112.after_ref.rest_ref = f32[16,128,128]{2,1,0:T(8,128)S(1)} custom-call(s32[1]{0:T(128)} %bitcast.core_ref, s32[6,16]{1,0:T(8,128)S(1)} %bitcast.9, s32[6,16]{1,0:T(8,128)S(1)} %bitcast.10, f32[6,16]{1,0:T(8,128)S(1)} %bitcast.11, f32[16]{0:T(128)S(1)} %copy-done.9, f32[16,128]{1,0:T(8,128)S(1)} %copy-done.3, bf16[32,128,128]{2,1,0:T(8,128)(2,1)S(1)} %copy-done, ...), custom_call_target="tpu_custom_call" | custom-call | flops 1000000000 | bytes 20971520 | tf_op jit(solution)/shard_map/pallas_call | solution.py:308
  50.1 0.7 collective-permute-done.7.array_ref
  50.8 7.0 %collective-permute-start.11 = (bf16[2048,2,128]{2,1,0:T(2,128)(2,1)S(1)}, bf16[2048,2,128]{2,1,0:T(2,128)(2,1)S(1)}, u32[]{:S(2)}, u32[]{:S(2)}) collective-permute-start(bf16[2048,2,128]{2,1,0:T(2,128)(2,1)S(1)} %shard_map.115.refs_3_), channel_id=1, source_target_pairs={{32,0},{33,1},{34,2},{35,3},{36,4},{37,5},{38,6},{39,7},{40,8},{41... | collective-permute-start | bytes 3145736 | tf_op jit(solution)/shard_map/ppermute | solution.py:49
  57.8 1.9 %collective-permute-start.10 = (bf16[2048,2,128]{2,1,0:T(2,128)(2,1)S(1)}, bf16[2048,2,128]{2,1,0:T(2,128)(2,1)S(1)}, u32[]{:S(2)}, u32[]{:S(2)}) collective-permute-start(bf16[2048,2,128]{2,1,0:T(2,128)(2,1)S(1)} %shard_map.114.refs_2_), channel_id=1, source_target_pairs={{32,0},{33,1},{34,2},{35,3},{36,4},{37,5},{38,6},{39,7},{40,8},{41... | collective-permute-start | bytes 3145736 | tf_op jit(solution)/shard_map/ppermute | solution.py:49
  59.8 2.5 %collective-permute-start.9 = (bf16[2048,2,128]{2,1,0:T(2,128)(2,1)S(1)}, bf16[2048,2,128]{2,1,0:T(2,128)(2,1)S(1)}, u32[]{:S(2)}, u32[]{:S(2)}) collective-permute-start(bf16[2048,2,128]{2,1,0:T(2,128)(2,1)S(1)} %shard_map.113.refs_1_), channel_id=1, source_target_pairs={{32,0},{33,1},{34,2},{35,3},{36,4},{37,5},{38,6},{39,7},{40,8},{41... | collective-permute-start | bytes 3145736 | tf_op jit(solution)/shard_map/ppermute | solution.py:49
  62.3 1.9 %collective-permute-start.12 = (bf16[1024,2,128]{2,1,0:T(2,128)(2,1)S(1)}, bf16[1024,2,128]{2,1,0:T(2,128)(2,1)S(1)}, u32[]{:S(2)}, u32[]{:S(2)}) collective-permute-start(bf16[1024,2,128]{2,1,0:T(2,128)(2,1)S(1)} %shard_map.116.refs_4_), channel_id=1, source_target_pairs={{32,0},{33,1},{34,2},{35,3},{36,4},{37,5},{38,6},{39,7},{40,8},{41... | collective-permute-start | bytes 1572872 | tf_op jit(solution)/shard_map/ppermute | solution.py:49
  64.3 1.9 %collective-permute-done.12.refs_8_ = bf16[1024,2,128]{2,1,0:T(2,128)(2,1)S(1)} collective-permute-done((bf16[1024,2,128]{2,1,0:T(2,128)(2,1)S(1)}, bf16[1024,2,128]{2,1,0:T(2,128)(2,1)S(1)}, u32[]{:S(2)}, u32[]{:S(2)}) %collective-permute-start.12) | collective-permute-done | bytes 524320 | tf_op jit(solution)/shard_map/ppermute | solution.py:49
  66.2 6.6 %shard_map.117 = bf16[16,128,128]{2,1,0:T(8,128)(2,1)} custom-call(s32[4096]{0:T(1024)S(1)} %bitcast.8, s32[16]{0:T(128)S(1)} %copy-done.8, bf16[16,256,128]{2,1,0:T(8,128)(2,1)S(1)} %copy-done.1, f32[16,128,128]{2,1,0:T(8,128)S(1)} %shard_map.112.after_ref.rest_ref, bf16[2048,2,128]{2,1,0:T(2,128)(2,1)S(1)} %get-tuple-element.7.after_ref.refs_0_, ...), custom_call_target="tpu_custom_call" | custom-call | flops 1000000000 | bytes 31457280 | tf_op jit(solution)/shard_map/pallas_call | solution.py:196
  (36 shorter events, 1.6 us)
Async XLA Ops:
  0.0 16.7 %copy-start.2 = (bf16[16,128,128]{2,1,0:T(8,128)(2,1)S(1)}, bf16[16,128,128]{2,1,0:T(8,128)(2,1)}, u32[]{:S(2)}) copy-start(bf16[16,128,128]{2,1,0:T(8,128)(2,1)} %tiles_ref.1) | copy-start | bytes 1572868
  1.1 25.4 %collective-permute-start.3 = (bf16[512,2,128]{2,1,0:T(2,128)(2,1)S(1)}, bf16[512,2,128]{2,1,0:T(2,128)(2,1)S(1)}, u32[]{:S(2)}, u32[]{:S(2)}) collective-permute-start(bf16[512,2,128]{2,1,0:T(2,128)(2,1)S(1)} %reshape.11.after_ref), channel_id=1, source_target_pairs={{16,0},{17,1},{18,2},{19,3},{21,4},{22,5},{23,6},{20,7},{25,8},{26... | collective-permute-start | bytes 786440 | tf_op jit(solution)/shard_map/ppermute | solution.py:49
  8.7 20.2 %collective-permute-start.2 = (bf16[512,2,128]{2,1,0:T(2,128)(2,1)S(1)}, bf16[512,2,128]{2,1,0:T(2,128)(2,1)S(1)}, u32[]{:S(2)}, u32[]{:S(2)}) collective-permute-start(bf16[512,2,128]{2,1,0:T(2,128)(2,1)S(1)} %reshape.11.after_ref), channel_id=1, source_target_pairs={{0,0},{1,1},{2,2},{3,3},{5,4},{6,5},{7,6},{4,7},{9,8},{10,9},{11,1... | collective-permute-start | bytes 786440 | tf_op jit(solution)/shard_map/ppermute | solution.py:49
  16.7 0.7 copy-start.7
  18.1 12.8 %collective-permute-start.1 = (bf16[16,128,128]{2,1,0:T(8,128)(2,1)S(1)}, bf16[16,128,128]{2,1,0:T(8,128)(2,1)S(1)}, u32[]{:S(2)}, u32[]{:S(2)}) collective-permute-start(bf16[16,128,128]{2,1,0:T(8,128)(2,1)S(1)} %shard_map.109.own_ref), channel_id=1, source_target_pairs={{32,0},{33,1},{34,2},{35,3},{36,4},{37,5},{38,6},{39,7},{40,8},{41... | collective-permute-start | bytes 1572872 | tf_op jit(solution)/shard_map/ppermute | solution.py:49
  20.1 11.9 %collective-permute-start = (bf16[16,128,128]{2,1,0:T(8,128)(2,1)S(1)}, bf16[16,128,128]{2,1,0:T(8,128)(2,1)S(1)}, u32[]{:S(2)}, u32[]{:S(2)}) collective-permute-start(bf16[16,128,128]{2,1,0:T(8,128)(2,1)S(1)} %shard_map.109.own_ref), channel_id=1, source_target_pairs={{480,0},{481,1},{482,2},{483,3},{484,4},{485,5},{486,6},{487,7},{4... | collective-permute-start | bytes 1572872 | tf_op jit(solution)/shard_map/ppermute | solution.py:49
  24.9 0.7 copy-start.10
  28.9 3.8 %collective-permute-start.4 = (bf16[1024,2,128]{2,1,0:T(2,128)(2,1)S(1)}, bf16[1024,2,128]{2,1,0:T(2,128)(2,1)S(1)}, u32[]{:S(2)}, u32[]{:S(2)}) collective-permute-start(bf16[1024,2,128]{2,1,0:T(2,128)(2,1)S(1)} %shard_map.110.own_ref), channel_id=1, source_target_pairs={{32,0},{33,1},{34,2},{35,3},{36,4},{37,5},{38,6},{39,7},{40,8},{41... | collective-permute-start | bytes 1572872 | tf_op jit(solution)/shard_map/ppermute | solution.py:49
  32.8 12.6 %copy-start = (bf16[32,128,128]{2,1,0:T(8,128)(2,1)S(1)}, bf16[32,128,128]{2,1,0:T(8,128)(2,1)}, u32[]{:S(2)}) copy-start(bf16[32,128,128]{2,1,0:T(8,128)(2,1)} %pool_hbm.1) | copy-start | bytes 3145732
  32.8 12.6 %copy-start.4 = (s32[16,6]{0,1:T(8,128)S(1)}, s32[16,6]{0,1:T(8,128)}, u32[]{:S(2)}) copy-start(s32[16,6]{0,1:T(8,128)} %param.18) | copy-start | bytes 1156
  32.8 12.6 %copy-start.5 = (s32[16,6]{0,1:T(8,128)S(1)}, s32[16,6]{0,1:T(8,128)}, u32[]{:S(2)}) copy-start(s32[16,6]{0,1:T(8,128)} %param.19) | copy-start | bytes 1156
  32.8 12.6 %copy-start.6 = (f32[16,6]{0,1:T(8,128)S(1)}, f32[16,6]{0,1:T(8,128)}, u32[]{:S(2)}) copy-start(f32[16,6]{0,1:T(8,128)} %param.20) | copy-start | bytes 1156
  32.9 12.4 %copy-start.3 = (f32[16,128]{1,0:T(8,128)S(1)}, f32[16,128]{1,0:T(8,128)}, u32[]{:S(2)}) copy-start(f32[16,128]{1,0:T(8,128)} %energy_hbm.1) | copy-start | bytes 24580
  32.9 17.9 %collective-permute-start.7 = (bf16[2048,2,128]{2,1,0:T(2,128)(2,1)S(1)}, bf16[2048,2,128]{2,1,0:T(2,128)(2,1)S(1)}, u32[]{:S(2)}, u32[]{:S(2)}) collective-permute-start(bf16[2048,2,128]{2,1,0:T(2,128)(2,1)S(1)} %get-tuple-element.7.after_ref.refs_0_), channel_id=1, source_target_pairs={{4,0},{5,1},{6,2},{7,3},{8,4},{9,5},{10,6},{11,7},{12,8},{13,9},{1... | collective-permute-start | bytes 3145736 | tf_op jit(solution)/shard_map/ppermute | solution.py:49
  35.7 22.1 %collective-permute-start.6 = (bf16[2048,2,128]{2,1,0:T(2,128)(2,1)S(1)}, bf16[2048,2,128]{2,1,0:T(2,128)(2,1)S(1)}, u32[]{:S(2)}, u32[]{:S(2)}) collective-permute-start(bf16[2048,2,128]{2,1,0:T(2,128)(2,1)S(1)} %get-tuple-element.7.after_ref.refs_0_), channel_id=1, source_target_pairs={{64,0},{65,1},{66,2},{67,3},{68,4},{69,5},{70,6},{71,7},{72,8},{73... | collective-permute-start | bytes 3145736 | tf_op jit(solution)/shard_map/ppermute | solution.py:49
  38.9 20.8 %collective-permute-start.5 = (bf16[2048,2,128]{2,1,0:T(2,128)(2,1)S(1)}, bf16[2048,2,128]{2,1,0:T(2,128)(2,1)S(1)}, u32[]{:S(2)}, u32[]{:S(2)}) collective-permute-start(bf16[2048,2,128]{2,1,0:T(2,128)(2,1)S(1)} %get-tuple-element.7.after_ref.refs_0_), channel_id=1, source_target_pairs={{1,0},{2,1},{3,2},{0,3},{5,4},{6,5},{7,6},{4,7},{9,8},{10,9},{11,1... | collective-permute-start | bytes 3145736 | tf_op jit(solution)/shard_map/ppermute | solution.py:49
  40.9 21.5 %collective-permute-start.8 = (bf16[1024,2,128]{2,1,0:T(2,128)(2,1)S(1)}, bf16[1024,2,128]{2,1,0:T(2,128)(2,1)S(1)}, u32[]{:S(2)}, u32[]{:S(2)}) collective-permute-start(bf16[1024,2,128]{2,1,0:T(2,128)(2,1)S(1)} %get-tuple-element.8), channel_id=1, source_target_pairs={{68,0},{69,1},{70,2},{71,3},{72,4},{73,5},{74,6},{75,7},{76,8},{77... | collective-permute-start | bytes 1572872 | tf_op jit(solution)/shard_map/ppermute | solution.py:49
  45.3 0.7 copy-start.9
  50.8 15.4 %collective-permute-start.11 = (bf16[2048,2,128]{2,1,0:T(2,128)(2,1)S(1)}, bf16[2048,2,128]{2,1,0:T(2,128)(2,1)S(1)}, u32[]{:S(2)}, u32[]{:S(2)}) collective-permute-start(bf16[2048,2,128]{2,1,0:T(2,128)(2,1)S(1)} %shard_map.115.refs_3_), channel_id=1, source_target_pairs={{32,0},{33,1},{34,2},{35,3},{36,4},{37,5},{38,6},{39,7},{40,8},{41... | collective-permute-start | bytes 3145736 | tf_op jit(solution)/shard_map/ppermute | solution.py:49
  57.8 8.3 %collective-permute-start.10 = (bf16[2048,2,128]{2,1,0:T(2,128)(2,1)S(1)}, bf16[2048,2,128]{2,1,0:T(2,128)(2,1)S(1)}, u32[]{:S(2)}, u32[]{:S(2)}) collective-permute-start(bf16[2048,2,128]{2,1,0:T(2,128)(2,1)S(1)} %shard_map.114.refs_2_), channel_id=1, source_target_pairs={{32,0},{33,1},{34,2},{35,3},{36,4},{37,5},{38,6},{39,7},{40,8},{41... | collective-permute-start | bytes 3145736 | tf_op jit(solution)/shard_map/ppermute | solution.py:49
  59.8 6.4 %copy-start.1 = (bf16[16,256,128]{2,1,0:T(8,128)(2,1)S(1)}, bf16[16,256,128]{2,1,0:T(8,128)(2,1)}, u32[]{:S(2)}) copy-start(bf16[16,256,128]{2,1,0:T(8,128)(2,1)} %maps_ref.1) | copy-start | bytes 3145732
  59.8 6.4 %copy-start.8 = (s32[16]{0:T(128)S(1)}, s32[16]{0:T(128)}, u32[]{:S(2)}) copy-start(s32[16]{0:T(128)} %count_ref.3) | copy-start | bytes 196
  59.8 6.4 %collective-permute-start.9 = (bf16[2048,2,128]{2,1,0:T(2,128)(2,1)S(1)}, bf16[2048,2,128]{2,1,0:T(2,128)(2,1)S(1)}, u32[]{:S(2)}, u32[]{:S(2)}) collective-permute-start(bf16[2048,2,128]{2,1,0:T(2,128)(2,1)S(1)} %shard_map.113.refs_1_), channel_id=1, source_target_pairs={{32,0},{33,1},{34,2},{35,3},{36,4},{37,5},{38,6},{39,7},{40,8},{41... | collective-permute-start | bytes 3145736 | tf_op jit(solution)/shard_map/ppermute | solution.py:49
  62.3 3.8 %collective-permute-start.12 = (bf16[1024,2,128]{2,1,0:T(2,128)(2,1)S(1)}, bf16[1024,2,128]{2,1,0:T(2,128)(2,1)S(1)}, u32[]{:S(2)}, u32[]{:S(2)}) collective-permute-start(bf16[1024,2,128]{2,1,0:T(2,128)(2,1)S(1)} %shard_map.116.refs_4_), channel_id=1, source_target_pairs={{32,0},{33,1},{34,2},{35,3},{36,4},{37,5},{38,6},{39,7},{40,8},{41... | collective-permute-start | bytes 1572872 | tf_op jit(solution)/shard_map/ppermute | solution.py:49

commit v4 on v3

--- a/solution.py
+++ b/solution.py
@@ -12,7 +12,6 @@
 SMEM = pl.BlockSpec(memory_space=pltpu.SMEM)
 VMEM = pl.BlockSpec(memory_space=pltpu.VMEM)
 ANY = pl.BlockSpec(memory_space=pl.ANY)
-HBM = pl.BlockSpec(memory_space=pltpu.HBM)
 
 FETCH = ((0, 2), (1, 3))
 TILT = 2
@@ -200,7 +199,7 @@
         out_specs=VMEM,
         scratch_shapes=[
             pltpu.VMEM((table_rows, 2, width // 2), jnp.bfloat16),
-            pltpu.VMEM((place.shape[0] * 2, width // 2), jnp.float32),
+            pltpu.VMEM((place.shape[0] * 2 + 16, width // 2), jnp.float32),
             pltpu.SemaphoreType.DMA((len(pieces),)),
         ],
         compiler_params=pltpu.CompilerParams(vmem_limit_bytes=24 * 2**20),
@@ -225,7 +224,7 @@
     return pl.pallas_call(
         mask_kernel,
         out_shape=jax.ShapeDtypeStruct(tiles.shape, tiles.dtype),
-        in_specs=[SMEM, HBM, ANY],
+        in_specs=[SMEM, ANY, ANY],
         out_specs=VMEM,
         scratch_shapes=[pltpu.VMEM(tiles.shape, tiles.dtype), pltpu.SemaphoreType.DMA(())],
         compiler_params=pltpu.CompilerParams(vmem_limit_bytes=4 * 2**20),
@@ -308,7 +307,7 @@
     return pl.pallas_call(
         couple_kernel,
         out_shape=jax.ShapeDtypeStruct((pairs, tile, tile), jnp.float32),
-        in_specs=[SMEM] + [HBM] * 6 + [ANY] * 4,
+        in_specs=[SMEM] + [ANY] * 10,
         out_specs=VMEM,
         scratch_shapes=[pltpu.SMEM(array.shape, array.dtype) for array in small]
         + [

time: 73.4 us -> 73.3 us (level)
  no operation moved by 1% of the time
where the time goes in v4:
time: 73.3 us; the launch traced here: 72.8 us
  starting transfers between devices  49.9 us (68%)
  Pallas kernels  11.7 us (16%)
  waiting for transfers between devices  7.61 us (10%)
  local copies, waits for them, and re-layouts  3.06 us (4%)
    ppermute x13, starting transfers between devices, send(): return lax.ppermute(array, AXES, pattern)  49.9 us
    ppermute x13, waiting for transfers between devices, send(): return lax.ppermute(array, AXES, pattern)  7.61 us
    pallas_call x1, Pallas kernels, exchange(): pl.pallas_call(functools.partial(exchange_kernel, len(pieces)), out_shape...  6.63 us
    pallas_call x1, Pallas kernels, couple(): pl.pallas_call(couple_kernel, out_shape=jax.ShapeDtypeStruct((pairs, tile...  4.15 us
    unnamed x23, local copies, waits for them, and re-layouts  1.99 us
  transfers between devices with their start and end apart: 13, of which 6 were waited for; matrix products, arithmetic and copies ran while one was open for 0% of the time, Pallas kernels for 7%

profile of v4, /device:TPU:1, one launch (start us, length us, event | category | flops | bytes accessed | tf_op | source)
XLA Modules:
  0.0 72.8 jit_solution(11957577790352802428)
XLA Ops:
  0.0 1.1 %reshape.11.after_ref = bf16[512,2,128]{2,1,0:T(2,128)(2,1)S(1)} reshape(bf16[512,256]{1,0:T(8,128)(2,1)} %param.11) | data formatting | bytes 524288 | tf_op jit(solution)/shard_map/reshape | solution.py:341
  1.1 7.6 %collective-permute-start.3 = (bf16[512,2,128]{2,1,0:T(2,128)(2,1)S(1)}, bf16[512,2,128]{2,1,0:T(2,128)(2,1)S(1)}, u32[]{:S(2)}, u32[]{:S(2)}) collective-permute-start(bf16[512,2,128]{2,1,0:T(2,128)(2,1)S(1)} %reshape.11.after_ref), channel_id=1, source_target_pairs={{16,0},{17,1},{18,2},{19,3},{21,4},{22,5},{23,6},{20,7},{25,8},{26... | collective-permute-start | bytes 786440 | tf_op jit(solution)/shard_map/ppermute | solution.py:48
  8.7 8.0 %collective-permute-start.2 = (bf16[512,2,128]{2,1,0:T(2,128)(2,1)S(1)}, bf16[512,2,128]{2,1,0:T(2,128)(2,1)S(1)}, u32[]{:S(2)}, u32[]{:S(2)}) collective-permute-start(bf16[512,2,128]{2,1,0:T(2,128)(2,1)S(1)} %reshape.11.after_ref), channel_id=1, source_target_pairs={{0,0},{1,1},{2,2},{3,3},{5,4},{6,5},{7,6},{4,7},{9,8},{10,9},{11,1... | collective-permute-start | bytes 786440 | tf_op jit(solution)/shard_map/ppermute | solution.py:48
  17.4 0.7 %shard_map.109.own_ref = bf16[16,128,128]{2,1,0:T(8,128)(2,1)S(1)} custom-call(s32[16]{0:T(128)S(1)} %copy-done.7, bf16[16,128,128]{2,1,0:T(8,128)(2,1)S(1)} %copy-done.2, bf16[512,2,128]{2,1,0:T(2,128)(2,1)S(1)} %reshape.11.after_ref), custom_call_target="tpu_custom_call" | custom-call | flops 1000000 | bytes 1048576 | tf_op jit(solution)/shard_map/pallas_call | solution.py:224
  18.1 1.9 %collective-permute-start.1 = (bf16[16,128,128]{2,1,0:T(8,128)(2,1)S(1)}, bf16[16,128,128]{2,1,0:T(8,128)(2,1)S(1)}, u32[]{:S(2)}, u32[]{:S(2)}) collective-permute-start(bf16[16,128,128]{2,1,0:T(8,128)(2,1)S(1)} %shard_map.109.own_ref), channel_id=1, source_target_pairs={{32,0},{33,1},{34,2},{35,3},{36,4},{37,5},{38,6},{39,7},{40,8},{41... | collective-permute-start | bytes 1572872 | tf_op jit(solution)/shard_map/ppermute | solution.py:48
  20.1 4.8 %collective-permute-start = (bf16[16,128,128]{2,1,0:T(8,128)(2,1)S(1)}, bf16[16,128,128]{2,1,0:T(8,128)(2,1)S(1)}, u32[]{:S(2)}, u32[]{:S(2)}) collective-permute-start(bf16[16,128,128]{2,1,0:T(8,128)(2,1)S(1)} %shard_map.109.own_ref), channel_id=1, source_target_pairs={{480,0},{481,1},{482,2},{483,3},{484,4},{485,5},{486,6},{487,7},{4... | collective-permute-start | bytes 1572872 | tf_op jit(solution)/shard_map/ppermute | solution.py:48
  24.9 0.7 copy-done.10
  25.7 0.8 %collective-permute-done.3.refs_1_ = bf16[512,2,128]{2,1,0:T(2,128)(2,1)S(1)} collective-permute-done((bf16[512,2,128]{2,1,0:T(2,128)(2,1)S(1)}, bf16[512,2,128]{2,1,0:T(2,128)(2,1)S(1)}, u32[]{:S(2)}, u32[]{:S(2)}) %collective-permute-start.3) | collective-permute-done | bytes 262176 | tf_op jit(solution)/shard_map/ppermute | solution.py:48
  26.5 2.4 %collective-permute-done.2.refs_0_ = bf16[512,2,128]{2,1,0:T(2,128)(2,1)S(1)} collective-permute-done((bf16[512,2,128]{2,1,0:T(2,128)(2,1)S(1)}, bf16[512,2,128]{2,1,0:T(2,128)(2,1)S(1)}, u32[]{:S(2)}, u32[]{:S(2)}) %collective-permute-start.2) | collective-permute-done | bytes 262176 | tf_op jit(solution)/shard_map/ppermute | solution.py:48
  28.9 1.9 %collective-permute-start.4 = (bf16[1024,2,128]{2,1,0:T(2,128)(2,1)S(1)}, bf16[1024,2,128]{2,1,0:T(2,128)(2,1)S(1)}, u32[]{:S(2)}, u32[]{:S(2)}) collective-permute-start(bf16[1024,2,128]{2,1,0:T(2,128)(2,1)S(1)} %shard_map.110.own_ref), channel_id=1, source_target_pairs={{32,0},{33,1},{34,2},{35,3},{36,4},{37,5},{38,6},{39,7},{40,8},{41... | collective-permute-start | bytes 1572872 | tf_op jit(solution)/shard_map/ppermute | solution.py:48
  30.9 1.1 %collective-permute-done.refs_0_.outside_ref = bf16[16,128,128]{2,1,0:T(8,128)(2,1)S(1)} collective-permute-done((bf16[16,128,128]{2,1,0:T(8,128)(2,1)S(1)}, bf16[16,128,128]{2,1,0:T(8,128)(2,1)S(1)}, u32[]{:S(2)}, u32[]{:S(2)}) %collective-permute-start) | collective-permute-done | bytes 524320 | tf_op jit(solution)/shard_map/ppermute | solution.py:48
  32.0 0.8 %collective-permute-done.4.partner_ref = bf16[1024,2,128]{2,1,0:T(2,128)(2,1)S(1)} collective-permute-done((bf16[1024,2,128]{2,1,0:T(2,128)(2,1)S(1)}, bf16[1024,2,128]{2,1,0:T(2,128)(2,1)S(1)}, u32[]{:S(2)}, u32[]{:S(2)}) %collective-permute-start.4) | collective-permute-done | bytes 524320 | tf_op jit(solution)/shard_map/ppermute | solution.py:48
  32.9 2.7 %collective-permute-start.7 = (bf16[2048,2,128]{2,1,0:T(2,128)(2,1)S(1)}, bf16[2048,2,128]{2,1,0:T(2,128)(2,1)S(1)}, u32[]{:S(2)}, u32[]{:S(2)}) collective-permute-start(bf16[2048,2,128]{2,1,0:T(2,128)(2,1)S(1)} %get-tuple-element.7.after_ref.refs_0_), channel_id=1, source_target_pairs={{4,0},{5,1},{6,2},{7,3},{8,4},{9,5},{10,6},{11,7},{12,8},{13,9},{1... | collective-permute-start | bytes 3145736 | tf_op jit(solution)/shard_map/ppermute | solution.py:48
  35.7 3.3 %collective-permute-start.6 = (bf16[2048,2,128]{2,1,0:T(2,128)(2,1)S(1)}, bf16[2048,2,128]{2,1,0:T(2,128)(2,1)S(1)}, u32[]{:S(2)}, u32[]{:S(2)}) collective-permute-start(bf16[2048,2,128]{2,1,0:T(2,128)(2,1)S(1)} %get-tuple-element.7.after_ref.refs_0_), channel_id=1, source_target_pairs={{64,0},{65,1},{66,2},{67,3},{68,4},{69,5},{70,6},{71,7},{72,8},{73... | collective-permute-start | bytes 3145736 | tf_op jit(solution)/shard_map/ppermute | solution.py:48
  38.9 1.9 %collective-permute-start.5 = (bf16[2048,2,128]{2,1,0:T(2,128)(2,1)S(1)}, bf16[2048,2,128]{2,1,0:T(2,128)(2,1)S(1)}, u32[]{:S(2)}, u32[]{:S(2)}) collective-permute-start(bf16[2048,2,128]{2,1,0:T(2,128)(2,1)S(1)} %get-tuple-element.7.after_ref.refs_0_), channel_id=1, source_target_pairs={{1,0},{2,1},{3,2},{0,3},{5,4},{6,5},{7,6},{4,7},{9,8},{10,9},{11,1... | collective-permute-start | bytes 3145736 | tf_op jit(solution)/shard_map/ppermute | solution.py:48
  40.9 4.4 %collective-permute-start.8 = (bf16[1024,2,128]{2,1,0:T(2,128)(2,1)S(1)}, bf16[1024,2,128]{2,1,0:T(2,128)(2,1)S(1)}, u32[]{:S(2)}, u32[]{:S(2)}) collective-permute-start(bf16[1024,2,128]{2,1,0:T(2,128)(2,1)S(1)} %get-tuple-element.8), channel_id=1, source_target_pairs={{68,0},{69,1},{70,2},{71,3},{72,4},{73,5},{74,6},{75,7},{76,8},{77... | collective-permute-start | bytes 1572872 | tf_op jit(solution)/shard_map/ppermute | solution.py:48
  46.0 4.1 %shard_map.112.after_ref.rest_ref = f32[16,128,128]{2,1,0:T(8,128)S(1)} custom-call(s32[1]{0:T(128)} %bitcast.core_ref, s32[6,16]{1,0:T(8,128)S(1)} %bitcast.9, s32[6,16]{1,0:T(8,128)S(1)} %bitcast.10, f32[6,16]{1,0:T(8,128)S(1)} %bitcast.11, f32[16]{0:T(128)S(1)} %copy-done.9, f32[16,128]{1,0:T(8,128)S(1)} %copy-done.3, bf16[32,128,128]{2,1,0:T(8,128)(2,1)S(1)} %copy-done, ...), custom_call_target="tpu_custom_call" | custom-call | flops 1000000000 | bytes 20971520 | tf_op jit(solution)/shard_map/pallas_call | solution.py:307
  50.1 0.7 collective-permute-done.7.array_ref
  50.8 7.0 %collective-permute-start.11 = (bf16[2048,2,128]{2,1,0:T(2,128)(2,1)S(1)}, bf16[2048,2,128]{2,1,0:T(2,128)(2,1)S(1)}, u32[]{:S(2)}, u32[]{:S(2)}) collective-permute-start(bf16[2048,2,128]{2,1,0:T(2,128)(2,1)S(1)} %shard_map.115.refs_3_), channel_id=1, source_target_pairs={{32,0},{33,1},{34,2},{35,3},{36,4},{37,5},{38,6},{39,7},{40,8},{41... | collective-permute-start | bytes 3145736 | tf_op jit(solution)/shard_map/ppermute | solution.py:48
  57.8 1.9 %collective-permute-start.10 = (bf16[2048,2,128]{2,1,0:T(2,128)(2,1)S(1)}, bf16[2048,2,128]{2,1,0:T(2,128)(2,1)S(1)}, u32[]{:S(2)}, u32[]{:S(2)}) collective-permute-start(bf16[2048,2,128]{2,1,0:T(2,128)(2,1)S(1)} %shard_map.114.refs_2_), channel_id=1, source_target_pairs={{32,0},{33,1},{34,2},{35,3},{36,4},{37,5},{38,6},{39,7},{40,8},{41... | collective-permute-start | bytes 3145736 | tf_op jit(solution)/shard_map/ppermute | solution.py:48
  59.8 2.5 %collective-permute-start.9 = (bf16[2048,2,128]{2,1,0:T(2,128)(2,1)S(1)}, bf16[2048,2,128]{2,1,0:T(2,128)(2,1)S(1)}, u32[]{:S(2)}, u32[]{:S(2)}) collective-permute-start(bf16[2048,2,128]{2,1,0:T(2,128)(2,1)S(1)} %shard_map.113.refs_1_), channel_id=1, source_target_pairs={{32,0},{33,1},{34,2},{35,3},{36,4},{37,5},{38,6},{39,7},{40,8},{41... | collective-permute-start | bytes 3145736 | tf_op jit(solution)/shard_map/ppermute | solution.py:48
  62.3 1.9 %collective-permute-start.12 = (bf16[1024,2,128]{2,1,0:T(2,128)(2,1)S(1)}, bf16[1024,2,128]{2,1,0:T(2,128)(2,1)S(1)}, u32[]{:S(2)}, u32[]{:S(2)}) collective-permute-start(bf16[1024,2,128]{2,1,0:T(2,128)(2,1)S(1)} %shard_map.116.refs_4_), channel_id=1, source_target_pairs={{32,0},{33,1},{34,2},{35,3},{36,4},{37,5},{38,6},{39,7},{40,8},{41... | collective-permute-start | bytes 1572872 | tf_op jit(solution)/shard_map/ppermute | solution.py:48
  64.3 1.9 %collective-permute-done.12.refs_8_ = bf16[1024,2,128]{2,1,0:T(2,128)(2,1)S(1)} collective-permute-done((bf16[1024,2,128]{2,1,0:T(2,128)(2,1)S(1)}, bf16[1024,2,128]{2,1,0:T(2,128)(2,1)S(1)}, u32[]{:S(2)}, u32[]{:S(2)}) %collective-permute-start.12) | collective-permute-done | bytes 524320 | tf_op jit(solution)/shard_map/ppermute | solution.py:48
  66.2 6.6 %shard_map.117 = bf16[16,128,128]{2,1,0:T(8,128)(2,1)} custom-call(s32[4096]{0:T(1024)S(1)} %bitcast.8, s32[16]{0:T(128)S(1)} %copy-done.8, bf16[16,256,128]{2,1,0:T(8,128)(2,1)S(1)} %copy-done.1, f32[16,128,128]{2,1,0:T(8,128)S(1)} %shard_map.112.after_ref.rest_ref, bf16[2048,2,128]{2,1,0:T(2,128)(2,1)S(1)} %get-tuple-element.7.after_ref.refs_0_, ...), custom_call_target="tpu_custom_call" | custom-call | flops 1000000000 | bytes 31457280 | tf_op jit(solution)/shard_map/pallas_call | solution.py:195
  (36 shorter events, 1.6 us)
Async XLA Ops:
  0.0 16.7 %copy-start.2 = (bf16[16,128,128]{2,1,0:T(8,128)(2,1)S(1)}, bf16[16,128,128]{2,1,0:T(8,128)(2,1)}, u32[]{:S(2)}) copy-start(bf16[16,128,128]{2,1,0:T(8,128)(2,1)} %tiles_ref.1) | copy-start | bytes 1572868
  1.1 25.4 %collective-permute-start.3 = (bf16[512,2,128]{2,1,0:T(2,128)(2,1)S(1)}, bf16[512,2,128]{2,1,0:T(2,128)(2,1)S(1)}, u32[]{:S(2)}, u32[]{:S(2)}) collective-permute-start(bf16[512,2,128]{2,1,0:T(2,128)(2,1)S(1)} %reshape.11.after_ref), channel_id=1, source_target_pairs={{16,0},{17,1},{18,2},{19,3},{21,4},{22,5},{23,6},{20,7},{25,8},{26... | collective-permute-start | bytes 786440 | tf_op jit(solution)/shard_map/ppermute | solution.py:48
  8.7 20.2 %collective-permute-start.2 = (bf16[512,2,128]{2,1,0:T(2,128)(2,1)S(1)}, bf16[512,2,128]{2,1,0:T(2,128)(2,1)S(1)}, u32[]{:S(2)}, u32[]{:S(2)}) collective-permute-start(bf16[512,2,128]{2,1,0:T(2,128)(2,1)S(1)} %reshape.11.after_ref), channel_id=1, source_target_pairs={{0,0},{1,1},{2,2},{3,3},{5,4},{6,5},{7,6},{4,7},{9,8},{10,9},{11,1... | collective-permute-start | bytes 786440 | tf_op jit(solution)/shard_map/ppermute | solution.py:48
  16.7 0.7 copy-start.7
  18.1 12.8 %collective-permute-start.1 = (bf16[16,128,128]{2,1,0:T(8,128)(2,1)S(1)}, bf16[16,128,128]{2,1,0:T(8,128)(2,1)S(1)}, u32[]{:S(2)}, u32[]{:S(2)}) collective-permute-start(bf16[16,128,128]{2,1,0:T(8,128)(2,1)S(1)} %shard_map.109.own_ref), channel_id=1, source_target_pairs={{32,0},{33,1},{34,2},{35,3},{36,4},{37,5},{38,6},{39,7},{40,8},{41... | collective-permute-start | bytes 1572872 | tf_op jit(solution)/shard_map/ppermute | solution.py:48
  20.1 11.9 %collective-permute-start = (bf16[16,128,128]{2,1,0:T(8,128)(2,1)S(1)}, bf16[16,128,128]{2,1,0:T(8,128)(2,1)S(1)}, u32[]{:S(2)}, u32[]{:S(2)}) collective-permute-start(bf16[16,128,128]{2,1,0:T(8,128)(2,1)S(1)} %shard_map.109.own_ref), channel_id=1, source_target_pairs={{480,0},{481,1},{482,2},{483,3},{484,4},{485,5},{486,6},{487,7},{4... | collective-permute-start | bytes 1572872 | tf_op jit(solution)/shard_map/ppermute | solution.py:48
  24.9 0.7 copy-start.10
  28.9 3.8 %collective-permute-start.4 = (bf16[1024,2,128]{2,1,0:T(2,128)(2,1)S(1)}, bf16[1024,2,128]{2,1,0:T(2,128)(2,1)S(1)}, u32[]{:S(2)}, u32[]{:S(2)}) collective-permute-start(bf16[1024,2,128]{2,1,0:T(2,128)(2,1)S(1)} %shard_map.110.own_ref), channel_id=1, source_target_pairs={{32,0},{33,1},{34,2},{35,3},{36,4},{37,5},{38,6},{39,7},{40,8},{41... | collective-permute-start | bytes 1572872 | tf_op jit(solution)/shard_map/ppermute | solution.py:48
  32.8 12.6 %copy-start = (bf16[32,128,128]{2,1,0:T(8,128)(2,1)S(1)}, bf16[32,128,128]{2,1,0:T(8,128)(2,1)}, u32[]{:S(2)}) copy-start(bf16[32,128,128]{2,1,0:T(8,128)(2,1)} %pool_hbm.1) | copy-start | bytes 3145732
  32.8 12.6 %copy-start.4 = (s32[16,6]{0,1:T(8,128)S(1)}, s32[16,6]{0,1:T(8,128)}, u32[]{:S(2)}) copy-start(s32[16,6]{0,1:T(8,128)} %param.18) | copy-start | bytes 1156
  32.8 12.6 %copy-start.5 = (s32[16,6]{0,1:T(8,128)S(1)}, s32[16,6]{0,1:T(8,128)}, u32[]{:S(2)}) copy-start(s32[16,6]{0,1:T(8,128)} %param.19) | copy-start | bytes 1156
  32.8 12.6 %copy-start.6 = (f32[16,6]{0,1:T(8,128)S(1)}, f32[16,6]{0,1:T(8,128)}, u32[]{:S(2)}) copy-start(f32[16,6]{0,1:T(8,128)} %param.20) | copy-start | bytes 1156
  32.9 12.4 %copy-start.3 = (f32[16,128]{1,0:T(8,128)S(1)}, f32[16,128]{1,0:T(8,128)}, u32[]{:S(2)}) copy-start(f32[16,128]{1,0:T(8,128)} %energy_hbm.1) | copy-start | bytes 24580
  32.9 17.9 %collective-permute-start.7 = (bf16[2048,2,128]{2,1,0:T(2,128)(2,1)S(1)}, bf16[2048,2,128]{2,1,0:T(2,128)(2,1)S(1)}, u32[]{:S(2)}, u32[]{:S(2)}) collective-permute-start(bf16[2048,2,128]{2,1,0:T(2,128)(2,1)S(1)} %get-tuple-element.7.after_ref.refs_0_), channel_id=1, source_target_pairs={{4,0},{5,1},{6,2},{7,3},{8,4},{9,5},{10,6},{11,7},{12,8},{13,9},{1... | collective-permute-start | bytes 3145736 | tf_op jit(solution)/shard_map/ppermute | solution.py:48
  35.7 22.1 %collective-permute-start.6 = (bf16[2048,2,128]{2,1,0:T(2,128)(2,1)S(1)}, bf16[2048,2,128]{2,1,0:T(2,128)(2,1)S(1)}, u32[]{:S(2)}, u32[]{:S(2)}) collective-permute-start(bf16[2048,2,128]{2,1,0:T(2,128)(2,1)S(1)} %get-tuple-element.7.after_ref.refs_0_), channel_id=1, source_target_pairs={{64,0},{65,1},{66,2},{67,3},{68,4},{69,5},{70,6},{71,7},{72,8},{73... | collective-permute-start | bytes 3145736 | tf_op jit(solution)/shard_map/ppermute | solution.py:48
  38.9 20.8 %collective-permute-start.5 = (bf16[2048,2,128]{2,1,0:T(2,128)(2,1)S(1)}, bf16[2048,2,128]{2,1,0:T(2,128)(2,1)S(1)}, u32[]{:S(2)}, u32[]{:S(2)}) collective-permute-start(bf16[2048,2,128]{2,1,0:T(2,128)(2,1)S(1)} %get-tuple-element.7.after_ref.refs_0_), channel_id=1, source_target_pairs={{1,0},{2,1},{3,2},{0,3},{5,4},{6,5},{7,6},{4,7},{9,8},{10,9},{11,1... | collective-permute-start | bytes 3145736 | tf_op jit(solution)/shard_map/ppermute | solution.py:48
  40.9 21.5 %collective-permute-start.8 = (bf16[1024,2,128]{2,1,0:T(2,128)(2,1)S(1)}, bf16[1024,2,128]{2,1,0:T(2,128)(2,1)S(1)}, u32[]{:S(2)}, u32[]{:S(2)}) collective-permute-start(bf16[1024,2,128]{2,1,0:T(2,128)(2,1)S(1)} %get-tuple-element.8), channel_id=1, source_target_pairs={{68,0},{69,1},{70,2},{71,3},{72,4},{73,5},{74,6},{75,7},{76,8},{77... | collective-permute-start | bytes 1572872 | tf_op jit(solution)/shard_map/ppermute | solution.py:48
  45.3 0.7 copy-start.9
  50.8 15.4 %collective-permute-start.11 = (bf16[2048,2,128]{2,1,0:T(2,128)(2,1)S(1)}, bf16[2048,2,128]{2,1,0:T(2,128)(2,1)S(1)}, u32[]{:S(2)}, u32[]{:S(2)}) collective-permute-start(bf16[2048,2,128]{2,1,0:T(2,128)(2,1)S(1)} %shard_map.115.refs_3_), channel_id=1, source_target_pairs={{32,0},{33,1},{34,2},{35,3},{36,4},{37,5},{38,6},{39,7},{40,8},{41... | collective-permute-start | bytes 3145736 | tf_op jit(solution)/shard_map/ppermute | solution.py:48
  57.8 8.3 %collective-permute-start.10 = (bf16[2048,2,128]{2,1,0:T(2,128)(2,1)S(1)}, bf16[2048,2,128]{2,1,0:T(2,128)(2,1)S(1)}, u32[]{:S(2)}, u32[]{:S(2)}) collective-permute-start(bf16[2048,2,128]{2,1,0:T(2,128)(2,1)S(1)} %shard_map.114.refs_2_), channel_id=1, source_target_pairs={{32,0},{33,1},{34,2},{35,3},{36,4},{37,5},{38,6},{39,7},{40,8},{41... | collective-permute-start | bytes 3145736 | tf_op jit(solution)/shard_map/ppermute | solution.py:48
  59.8 6.4 %copy-start.1 = (bf16[16,256,128]{2,1,0:T(8,128)(2,1)S(1)}, bf16[16,256,128]{2,1,0:T(8,128)(2,1)}, u32[]{:S(2)}) copy-start(bf16[16,256,128]{2,1,0:T(8,128)(2,1)} %maps_ref.1) | copy-start | bytes 3145732
  59.8 6.4 %copy-start.8 = (s32[16]{0:T(128)S(1)}, s32[16]{0:T(128)}, u32[]{:S(2)}) copy-start(s32[16]{0:T(128)} %count_ref.3) | copy-start | bytes 196
  59.8 6.4 %collective-permute-start.9 = (bf16[2048,2,128]{2,1,0:T(2,128)(2,1)S(1)}, bf16[2048,2,128]{2,1,0:T(2,128)(2,1)S(1)}, u32[]{:S(2)}, u32[]{:S(2)}) collective-permute-start(bf16[2048,2,128]{2,1,0:T(2,128)(2,1)S(1)} %shard_map.113.refs_1_), channel_id=1, source_target_pairs={{32,0},{33,1},{34,2},{35,3},{36,4},{37,5},{38,6},{39,7},{40,8},{41... | collective-permute-start | bytes 3145736 | tf_op jit(solution)/shard_map/ppermute | solution.py:48
  62.3 3.8 %collective-permute-start.12 = (bf16[1024,2,128]{2,1,0:T(2,128)(2,1)S(1)}, bf16[1024,2,128]{2,1,0:T(2,128)(2,1)S(1)}, u32[]{:S(2)}, u32[]{:S(2)}) collective-permute-start(bf16[1024,2,128]{2,1,0:T(2,128)(2,1)S(1)} %shard_map.116.refs_4_), channel_id=1, source_target_pairs={{32,0},{33,1},{34,2},{35,3},{36,4},{37,5},{38,6},{39,7},{40,8},{41... | collective-permute-start | bytes 1572872 | tf_op jit(solution)/shard_map/ppermute | solution.py:48
